TPU v7x, 32 devices: a whole 2x2x4 slice. The times are simulated.
32 devices in a mesh: ctx: 8 (over y, x, core), ch: 4 (over z).
Axes of the slice: x: 2, y: 2, z: 4, core: 2. Of those that a mesh axis runs over, the one named last changes fastest.
Arguments:
- tokens: bfloat16 [3072, 4096], P('ctx', 'ch'), may hold values from -2.5 to 2.5
- mr_gain: float32 [4096], replicated, may hold values from 0.1 to 1.9
- mr_inproj: bfloat16 [4096, 3, 4096], P('ctx', None, 'ch'), may hold values from -0.09375 to 0.09375
- mr_outproj: bfloat16 [4096, 4096], P('ch', 'ctx'), may hold values from -0.09375 to 0.09375
- mr_filter: float32 [128, 4096], P(None, 'ch'), may hold values from -0.5 to 0.5
- li_gain: float32 [4096], replicated, may hold values from 0.1 to 1.9
- li_inproj: bfloat16 [4096, 3, 4096], P('ctx', None, 'ch'), may hold values from -0.09375 to 0.09375
- li_outproj: bfloat16 [4096, 4096], P('ch', 'ctx'), may hold values from -0.09375 to 0.09375
- li_decay: float32 [16, 4096], P(None, 'ch'), may hold values from 1.6276042e-06 to 0.125
- li_residue: float32 [16, 4096], P(None, 'ch'), may hold values from -1 to 1
- doc_ids: int32 [3072], replicated, may hold values from 0 to 3, never falling along the last dimension, each value on 1 to 1536 neighbouring positions
Outputs:
- layer_out: bfloat16 [3072, 4096], P('ctx', 'ch')
Inputs may be any that keep to these rules, and one draw needn't show every extreme that they name: `doc_ids`: ids never fall along the sequence and every one of the 4 ids occurs.
All inputs are finite; a program needn't handle non-finite values.
Results may differ from a plain program's by a relative error of at most 0.03.
Values may be sent and summed in bfloat16 or wider, within the bound.
A program may use at most 192 MiB of HBM per device.

v0:
```python
import jax
import jax.numpy as jnp
from jax import lax
from jax.experimental import pallas as pl
from jax.experimental.pallas import tpu as pltpu
from jax.sharding import PartitionSpec as P

LANES = 128
ROWS = 8
VMEM_LIMIT = 40 * 1024 * 1024
vmem_spec = pl.BlockSpec(memory_space=pltpu.VMEM)
smem_spec = pl.BlockSpec(memory_space=pltpu.SMEM)


def gather_channels(stream):
    count, index = (lax.axis_size("ch"), lax.axis_index("ch"))
    channels = stream.shape[1]
    from_left, from_right = ([stream], [stream])
    for hop in range(1, count):
        up = [(i, i + 1) for i in range(hop - 1, count - 1)]
        down = [(i, i - 1) for i in range(1, count - hop + 1)]
        from_left.append(lax.ppermute(from_left[-1], "ch", up))
        from_right.append(lax.ppermute(from_right[-1], "ch", down))
    line = jnp.concatenate(from_left[:0:-1] + [stream] + from_right[1:], axis=1)
    return lax.dynamic_slice_in_dim(line, (count - 1 - index) * channels, count * channels, 1)


def scatter_channels(terms, stream):
    count, index = (lax.axis_size("ch"), lax.axis_index("ch"))
    channels = stream.shape[1]

    def block(number):
        begin = jnp.clip(number, 0, count - 1) * channels
        return lax.dynamic_slice_in_dim(terms, begin, channels, 1).astype(jnp.float32)

    total = block(index) + stream.astype(jnp.float32)
    right, left = (None, None)
    for far in range(count - 1, 0, -1):
        up = [(i, i + 1) for i in range(count - far)]
        down = [(i, i - 1) for i in range(far, count)]
        rightward, leftward = (block(index + far), block(index - far))
        if right is not None:
            rightward = rightward + right.astype(jnp.float32)
            leftward = leftward + left.astype(jnp.float32)
        right = lax.ppermute(rightward.astype(jnp.bfloat16), "ch", up)
        left = lax.ppermute(leftward.astype(jnp.bfloat16), "ch", down)
    return (total + right.astype(jnp.float32) + left.astype(jnp.float32)).astype(jnp.bfloat16)


def features_in(stream, gain, piece):
    whole = gather_channels(stream)
    floats = whole.astype(jnp.float32)
    scaled = lax.rsqrt(jnp.mean(floats * floats, axis=1, keepdims=True) + 1e-06)
    normed = (floats * scaled * gain[None, :]).astype(jnp.bfloat16)
    channels = piece.shape[2]
    flat = piece.reshape(piece.shape[0], 3 * channels)
    joined = jnp.dot(normed, flat, preferred_element_type=jnp.float32).astype(jnp.bfloat16)
    product = (
        joined[:, channels : 2 * channels].astype(jnp.float32)
        * joined[:, 2 * channels :].astype(jnp.float32)
    ).astype(jnp.bfloat16)
    return (joined[:, :channels], product)


def features_out(stream, query, mixed, piece):
    gated = (query.astype(jnp.float32) * mixed).astype(jnp.bfloat16)
    terms = jnp.dot(gated, piece, preferred_element_type=jnp.float32).astype(jnp.bfloat16)
    return scatter_channels(terms, stream)


def span_layout(shard_rows):
    ctx_count = lax.axis_size("ctx")
    ctx_index = lax.axis_index("ctx")
    span_rows = shard_rows // 2
    span_starts = jnp.stack([ctx_index * span_rows, (2 * ctx_count - 1 - ctx_index) * span_rows])
    return (ctx_count, ctx_index, span_rows, span_starts)


def short_kernel(docs, window, taps, out):
    span_rows = out.shape[1]
    reach = window.shape[1] - span_rows
    tile = out.shape[2:]

    def outputs(number, _):
        half = number // (span_rows // ROWS)
        row = pl.multiple_of((number % (span_rows // ROWS)) * ROWS, ROWS)
        first_doc = docs[half, reach + row]
        last_doc = docs[half, reach + row + ROWS - 1]

        def sources(step, sums):
            begin = row + step * ROWS
            base = reach - step * ROWS

            def load():
                source = [window[half, begin + b] for b in range(ROWS)]
                weight = [taps[base + d] for d in range(2 * ROWS - 1)]
                return source, weight

            def plain(sums):
                source, weight = load()
                sums = list(sums)
                for b in range(ROWS):
                    for a in range(ROWS):
                        sums[a] = sums[a] + source[b] * weight[a - b + ROWS - 1]
                return tuple(sums)

            def masked(sums):
                source, weight = load()
                sums = list(sums)
                for b in range(ROWS):
                    doc = docs[half, begin + b]
                    for a in range(ROWS):
                        same = jnp.where(doc == docs[half, reach + row + a], 1.0, 0.0)
                        sums[a] = sums[a] + (source[b] * same) * weight[a - b + ROWS - 1]
                return tuple(sums)

            return lax.cond(docs[half, begin] == last_doc, plain, masked, sums)

        def outside(step, skipped):
            return skipped + jnp.where(docs[half, row + step * ROWS + ROWS - 1] < first_doc, 1, 0)

        steps = reach // ROWS + 1
        skip = lax.fori_loop(0, steps, outside, jnp.int32(0))
        zero = jnp.zeros(tile, jnp.float32)
        sums = lax.fori_loop(skip, steps, sources, (zero,) * ROWS)
        for a in range(ROWS):
            out[half, row + a] = sums[a]
        return 0

    lax.fori_loop(0, 2 * (span_rows // ROWS), outputs, 0)


def short_mix(product, mr_filter, doc_ids):
    shard_rows, channels = product.shape
    ctx_count, ctx_index, span_rows, span_starts = span_layout(shard_rows)
    tap_count = mr_filter.shape[0]
    reach = -(-tap_count // ROWS) * ROWS
    halves = product.reshape(2, span_rows, channels)
    tails = halves[:, span_rows - reach :]
    up = [(i, i + 1) for i in range(ctx_count - 1)]
    down = [(i + 1, i) for i in range(ctx_count - 1)]
    before_lower = lax.ppermute(tails[0], "ctx", up)
    before_upper = lax.ppermute(tails[1], "ctx", down)
    before_upper = jnp.where(ctx_index == ctx_count - 1, tails[0], before_upper)
    window = jnp.concatenate([jnp.stack([before_lower, before_upper]), halves], 1)
    tile = (channels // LANES, LANES)
    window = window.astype(jnp.float32).reshape((2, reach + span_rows) + tile)
    places = span_starts[:, None] - reach + jnp.arange(reach + span_rows)[None, :]
    docs = jnp.where(places >= 0, jnp.take(doc_ids, jnp.clip(places, 0, None)), -1)
    taps = jnp.pad(mr_filter, ((ROWS - 1, reach + ROWS - tap_count), (0, 0)))
    taps = taps.reshape((taps.shape[0],) + tile)
    mixed = pl.pallas_call(
        short_kernel,
        out_shape=jax.ShapeDtypeStruct((2, span_rows) + tile, jnp.float32),
        in_specs=[smem_spec, vmem_spec, vmem_spec],
        out_specs=vmem_spec,
        compiler_params=pltpu.CompilerParams(vmem_limit_bytes=VMEM_LIMIT),
        cost_estimate=pl.CostEstimate(
            flops=2 * shard_rows * tap_count * channels,
            bytes_accessed=8 * shard_rows * channels,
            transcendentals=0,
        ),
        name="short_mix",
    )(docs, window, taps)
    return mixed.reshape(shard_rows, channels)


def states_kernel(follows, factor, values, finals):
    span_rows, modes = (values.shape[1], factor.shape[0])
    tile = values.shape[2:]
    for half in range(2):

        def step(row, states):
            value, keep = (values[half, row], follows[half, row])
            return tuple(states[m] * (factor[m] * keep) + value for m in range(modes))

        zero = jnp.zeros(tile, jnp.float32)
        states = lax.fori_loop(0, span_rows, step, (zero,) * modes)
        for m in range(modes):
            finals[half, m] = states[m]


def long_kernel(follows, factor, residue, initial, values, out):
    span_rows, modes = (values.shape[1], factor.shape[0])
    for half in range(2):

        def step(row, states):
            value, keep = (values[half, row], follows[half, row])
            states = tuple(states[m] * (factor[m] * keep) + value for m in range(modes))
            terms = [states[m] * residue[m] for m in range(modes)]
            while len(terms) > 1:
                pairs = [terms[k] + terms[k + 1] for k in range(0, len(terms) - 1, 2)]
                terms = pairs + terms[len(terms) - len(terms) % 2 :]
            out[half, row] = terms[0]
            return states

        lax.fori_loop(0, span_rows, step, tuple(initial[half, m] for m in range(modes)))


def long_mix(product, li_decay, li_residue, doc_ids):
    shard_rows, channels = product.shape
    ctx_count, ctx_index, span_rows, span_starts = span_layout(shard_rows)
    modes = li_decay.shape[0]
    tile = (channels // LANES, LANES)
    values = product.astype(jnp.float32).reshape((2, span_rows) + tile)
    decay = li_decay.reshape((modes,) + tile)
    residue = li_residue.reshape((modes,) + tile)
    factor = jnp.exp(-decay)
    places = span_starts[:, None] + jnp.arange(span_rows)[None, :]
    earlier = jnp.take(doc_ids, jnp.clip(places - 1, 0, None))
    follows = ((places > 0) & (jnp.take(doc_ids, places) == earlier)).astype(jnp.float32)
    params = pltpu.CompilerParams(vmem_limit_bytes=VMEM_LIMIT)
    flops = 2 * shard_rows * modes * channels
    finals = pl.pallas_call(
        states_kernel,
        out_shape=jax.ShapeDtypeStruct((2, modes) + tile, jnp.float32),
        in_specs=[smem_spec, vmem_spec, vmem_spec],
        out_specs=vmem_spec,
        compiler_params=params,
        cost_estimate=pl.CostEstimate(
            flops=flops, bytes_accessed=4 * shard_rows * channels, transcendentals=0
        ),
        name="block_states",
    )(follows, factor, values)
    before_docs = earlier[:, 0]
    initial = jnp.zeros((2, modes) + tile, jnp.float32)
    for shift in range(ctx_count):
        source = (ctx_index - shift) % ctx_count
        states = finals
        if shift:
            ring = [(i, (i + shift) % ctx_count) for i in range(ctx_count)]
            states = lax.ppermute(finals, "ctx", ring)
        for part, block in enumerate((source, 2 * ctx_count - 1 - source)):
            last = (block + 1) * span_rows - 1
            gap = span_starts - 1 - last
            keep = (gap >= 0) & (jnp.take(doc_ids, last) == before_docs)
            distance = jnp.where(keep, gap, 0).astype(jnp.float32)[:, None, None, None]
            weight = jnp.exp(-decay[None] * distance) * keep.astype(jnp.float32)[:, None, None, None]
            initial = initial + weight * states[part][None]
    mixed = pl.pallas_call(
        long_kernel,
        out_shape=jax.ShapeDtypeStruct((2, span_rows) + tile, jnp.float32),
        in_specs=[smem_spec] + [vmem_spec] * 4,
        out_specs=vmem_spec,
        compiler_params=params,
        cost_estimate=pl.CostEstimate(
            flops=2 * flops, bytes_accessed=8 * shard_rows * channels, transcendentals=0
        ),
        name="long_mix",
    )(follows, factor, residue, initial, values)
    return mixed.reshape(shard_rows, channels)


def body(
    tokens,
    mr_gain,
    mr_inproj,
    mr_outproj,
    mr_filter,
    li_gain,
    li_inproj,
    li_outproj,
    li_decay,
    li_residue,
    doc_ids,
):
    mr_in = lax.all_gather(mr_inproj, "ctx", axis=0, tiled=True)
    mr_out = lax.all_gather(mr_outproj, "ctx", axis=1, tiled=True)
    li_in = lax.all_gather(li_inproj, "ctx", axis=0, tiled=True)
    li_out = lax.all_gather(li_outproj, "ctx", axis=1, tiled=True)
    query, product = features_in(tokens, mr_gain, mr_in)
    stream = features_out(tokens, query, short_mix(product, mr_filter, doc_ids), mr_out)
    query, product = features_in(stream, li_gain, li_in)
    return features_out(stream, query, long_mix(product, li_decay, li_residue, doc_ids), li_out)


def solution(mesh):
    in_specs = (
        P("ctx", "ch"),
        P(),
        P("ctx", None, "ch"),
        P("ch", "ctx"),
        P(None, "ch"),
        P(),
        P("ctx", None, "ch"),
        P("ch", "ctx"),
        P(None, "ch"),
        P(None, "ch"),
        P(),
    )
    out_specs = P("ctx", "ch")
    return jax.shard_map(body, mesh=mesh, in_specs=in_specs, out_specs=out_specs, check_vma=False)
```

profile of v0, /device:TPU:14, one launch (start us, length us, event | category | flops | bytes accessed | tf_op | source)
XLA Modules:
  0.0 548.5 jit_solution(16064738592820307533)
XLA Ops:
  6.5 4.7 copy.12
  23.1 15.3 %collective-permute-done = bf16[384,1024]{1,0:T(8,128)(2,1)S(1)} collective-permute-done((bf16[384,1024]{1,0:T(8,128)(2,1)S(1)}, bf16[384,1024]{1,0:T(8,128)(2,1)S(1)}, u32[]{:S(2)}, u32[]{:S(2)}) %collective-permute-start) | collective-permute-done | bytes 786464 | tf_op jit(solution)/shard_map/ppermute | solution.py:22
  38.4 4.5 collective-permute-start.1
  44.9 13.0 %collective-permute-done.1 = bf16[384,1024]{1,0:T(8,128)(2,1)} collective-permute-done((bf16[384,1024]{1,0:T(8,128)(2,1)S(1)}, bf16[384,1024]{1,0:T(8,128)(2,1)}, u32[]{:S(2)}, u32[]{:S(2)}) %collective-permute-start.1) | collective-permute-done | bytes 786464 | tf_op jit(solution)/shard_map/ppermute | solution.py:22
  59.8 3.9 gather_fusion
  75.1 5.9 %collective-permute-done.5 = bf16[384,1024]{1,0:T(8,128)(2,1)S(1)} collective-permute-done((bf16[384,1024]{1,0:T(8,128)(2,1)}, bf16[384,1024]{1,0:T(8,128)(2,1)S(1)}, u32[]{:S(2)}, u32[]{:S(2)}) %collective-permute-start.5) | collective-permute-done | bytes 786464 | tf_op jit(solution)/shard_map/ppermute | solution.py:23
  84.5 57.3 %all-gather.5.cloned.1.call-done = bf16[4096,3,1024]{0,2,1:T(8,128)(2,1)} async-done(((bf16[512,3,1024]{0,2,1:T(8,128)(2,1)}), bf16[4096,3,1024]{0,2,1:T(8,128)(2,1)}) %all-gather.5.cloned.1.call-update) | async-done | bytes 25165840 | tf_op jit(solution)/shard_map/all_gather | solution.py:267
  141.9 15.7 %convolution_convert_fusion.3 = bf16[384,3072]{1,0:T(8,128)(2,1)S(1)} fusion(bf16[4096,3072]{0,1:T(8,128)(2,1)} %bitcast.135, f32[4096]{0:T(1024)S(1)} %copy-done.11, f32[384]{0:T(512)S(1)} %add_rsqrt_fusion.1, bf16[384,7168]{1,0:T(8,128)(2,1)} %constant_dynamic-update-slice_fusion, s32[]{:T(128)S(6)} %select_n.304), kind=kOutput, calls=%fused_computation.16 | convolution fusion | flops 9671147520 | bytes 30688772 | tf_op jit(solution)/shard_map/dot_general | solution.py:57
  162.9 4.4 collective-permute-done.7
  171.3 50.1 %short_mix.1 = f32[2,192,8,128]{3,2,1,0:T(8,128)S(1)} custom-call(s32[2,320]{1,0:T(2,128)S(1)} %compare_select_fusion.2.docs, f32[2,320,8,128]{3,2,1,0:T(8,128)S(1)} %maximum_convert_fusion.window, f32[143,8,128]{2,1,0:T(8,128)S(1)} %slice.215.taps), custom_call_target="tpu_custom_call" | custom-call | flops 100663296 | bytes 3145728 | tf_op jit(solution)/shard_map/short_mix/pallas_call | solution.py:152
  221.5 7.3 %convolution_convert_fusion.1 = bf16[384,4096]{1,0:T(8,128)(2,1)S(1)} fusion(bf16[1024,4096]{1,0:T(8,128)(2,1)} %all-gather.7.cloned.1.call-done, f32[48,8,8,128]{3,2,1,0:T(8,128)S(1)} %bitcast.122, bf16[384,3072]{1,0:T(8,128)(2,1)} %copy-done.3), kind=kOutput, calls=%fused_computation.14 | convolution fusion | flops 3223977984 | bytes 13893632 | tf_op jit(solution)/shard_map/dot_general | solution.py:67
  234.7 12.2 %collective-permute-done.8 = bf16[384,1024]{1,0:T(8,128)(2,1)} collective-permute-done((bf16[384,1024]{1,0:T(8,128)(2,1)}, bf16[384,1024]{1,0:T(8,128)(2,1)}, u32[]{:S(2)}, u32[]{:S(2)}) %collective-permute-start.8) | collective-permute-done | bytes 786464 | tf_op jit(solution)/shard_map/ppermute | solution.py:45
  251.3 12.3 %collective-permute-done.9 = bf16[384,1024]{1,0:T(8,128)(2,1)} collective-permute-done((bf16[384,1024]{1,0:T(8,128)(2,1)}, bf16[384,1024]{1,0:T(8,128)(2,1)}, u32[]{:S(2)}, u32[]{:S(2)}) %collective-permute-start.9) | collective-permute-done | bytes 786464 | tf_op jit(solution)/shard_map/ppermute | solution.py:45
  268.7 4.6 collective-permute-start.10
  273.3 11.0 %collective-permute-done.12 = bf16[384,1024]{1,0:T(8,128)(2,1)} collective-permute-done((bf16[384,1024]{1,0:T(8,128)(2,1)}, bf16[384,1024]{1,0:T(8,128)(2,1)}, u32[]{:S(2)}, u32[]{:S(2)}) %collective-permute-start.12) | collective-permute-done | bytes 786464 | tf_op jit(solution)/shard_map/ppermute | solution.py:46
  288.5 12.3 %collective-permute-done.13 = bf16[384,1024]{1,0:T(8,128)(2,1)} collective-permute-done((bf16[384,1024]{1,0:T(8,128)(2,1)}, bf16[384,1024]{1,0:T(8,128)(2,1)}, u32[]{:S(2)}, u32[]{:S(2)}) %collective-permute-start.13) | collective-permute-done | bytes 786464 | tf_op jit(solution)/shard_map/ppermute | solution.py:46
  329.0 14.8 %collective-permute-done.17 = bf16[384,1024]{1,0:T(8,128)(2,1)S(1)} collective-permute-done((bf16[384,1024]{1,0:T(8,128)(2,1)}, bf16[384,1024]{1,0:T(8,128)(2,1)S(1)}, u32[]{:S(2)}, u32[]{:S(2)}) %collective-permute-start.17) | collective-permute-done | bytes 786464 | tf_op jit(solution)/shard_map/ppermute | solution.py:23
  343.8 4.3 collective-permute-start.18
  349.1 16.9 %collective-permute-done.18 = bf16[384,1024]{1,0:T(8,128)(2,1)S(1)} collective-permute-done((bf16[384,1024]{1,0:T(8,128)(2,1)S(1)}, bf16[384,1024]{1,0:T(8,128)(2,1)S(1)}, u32[]{:S(2)}, u32[]{:S(2)}) %collective-permute-start.18) | collective-permute-done | bytes 786464 | tf_op jit(solution)/shard_map/ppermute | solution.py:23
  366.0 4.6 collective-permute-start.19
  372.1 7.7 %collective-permute-done.19 = bf16[384,1024]{1,0:T(8,128)(2,1)S(1)} collective-permute-done((bf16[384,1024]{1,0:T(8,128)(2,1)S(1)}, bf16[384,1024]{1,0:T(8,128)(2,1)S(1)}, u32[]{:S(2)}, u32[]{:S(2)}) %collective-permute-start.19) | collective-permute-done | bytes 786464 | tf_op jit(solution)/shard_map/ppermute | solution.py:23
  383.1 15.7 %convolution_convert_fusion.2 = bf16[384,3072]{1,0:T(8,128)(2,1)S(1)} fusion(bf16[4096,3072]{0,1:T(8,128)(2,1)} %bitcast.134, f32[4096]{0:T(1024)S(1)} %copy-done.12, f32[384]{0:T(512)S(1)} %add_rsqrt_fusion, bf16[384,7168]{1,0:T(8,128)(2,1)} %copy-done.6, s32[]{:T(128)S(6)} %select_n.304), kind=kOutput, calls=%fused_computation.15 | convolution fusion | flops 9671147520 | bytes 30688772 | tf_op jit(solution)/shard_map/dot_general | solution.py:57
  400.2 5.4 block_states.1
  405.7 22.3 %collective-permute-start.22 = (f32[2,16,8,128]{3,2,1,0:T(8,128)S(1)}, f32[2,16,8,128]{3,2,1,0:T(8,128)S(1)}, u32[]{:S(2)}, u32[]{:S(2)}) collective-permute-start(f32[2,16,8,128]{3,2,1,0:T(8,128)S(1)} %block_states.1), channel_id=1, source_target_pairs={{0,12},{4,16},{8,20},{12,24},{16,28},{20,0},{24,4},{28,8},{1,13},{... | collective-permute-start | bytes 393224 | tf_op jit(solution)/shard_map/ppermute | solution.py:232
  433.5 6.2 %collective-permute-done.24 = f32[2,16,8,128]{3,2,1,0:T(8,128)S(1)} collective-permute-done((f32[2,16,8,128]{3,2,1,0:T(8,128)S(1)}, f32[2,16,8,128]{3,2,1,0:T(8,128)S(1)}, u32[]{:S(2)}, u32[]{:S(2)}) %collective-permute-start.24) | collective-permute-done | bytes 131104 | tf_op jit(solution)/shard_map/ppermute | solution.py:232
  440.5 7.5 %long_mix.1 = f32[2,192,8,128]{3,2,1,0:T(8,128)S(1)} custom-call(f32[2,192]{1,0:T(2,128)S(1)} %and_convert_fusion.follows, f32[16,8,128]{2,1,0:T(8,128)S(1)} %bitcast_exponential_fusion.factor, f32[16,8,128]{2,1,0:T(8,128)S(1)} %bitcast.123, f32[2,16,8,128]{3,2,1,0:T(8,128)S(1)} %multiply_add_fusion.initial, f32[2,192,8,128]{3,2,1,0:T(8,128)S(1)} %bitcast.120), custom_call_target="tpu_custom_call" | custom-call | flops 25165824 | bytes 3145728 | tf_op jit(solution)/shard_map/long_mix/pallas_call | solution.py:240
  448.1 7.1 %convolution_convert_fusion = bf16[384,4096]{1,0:T(8,128)(2,1)S(1)} fusion(bf16[1024,4096]{1,0:T(8,128)(2,1)} %all-gather.11.cloned.1.call-done, f32[48,8,8,128]{3,2,1,0:T(8,128)S(1)} %bitcast.121, bf16[384,3072]{1,0:T(8,128)(2,1)} %copy-done.7), kind=kOutput, calls=%fused_computation.13 | convolution fusion | flops 3223977984 | bytes 13893632 | tf_op jit(solution)/shard_map/dot_general | solution.py:67
  457.3 20.0 %collective-permute-done.27 = bf16[384,1024]{1,0:T(8,128)(2,1)S(1)} collective-permute-done((bf16[384,1024]{1,0:T(8,128)(2,1)S(1)}, bf16[384,1024]{1,0:T(8,128)(2,1)S(1)}, u32[]{:S(2)}, u32[]{:S(2)}) %collective-permute-start.27) | collective-permute-done | bytes 786464 | tf_op jit(solution)/shard_map/ppermute | solution.py:45
  479.6 19.2 %collective-permute-done.28 = bf16[384,1024]{1,0:T(8,128)(2,1)S(1)} collective-permute-done((bf16[384,1024]{1,0:T(8,128)(2,1)S(1)}, bf16[384,1024]{1,0:T(8,128)(2,1)S(1)}, u32[]{:S(2)}, u32[]{:S(2)}) %collective-permute-start.28) | collective-permute-done | bytes 786464 | tf_op jit(solution)/shard_map/ppermute | solution.py:45
  500.8 4.6 collective-permute-start.29
  505.4 14.4 %collective-permute-done.31 = bf16[384,1024]{1,0:T(8,128)(2,1)S(1)} collective-permute-done((bf16[384,1024]{1,0:T(8,128)(2,1)S(1)}, bf16[384,1024]{1,0:T(8,128)(2,1)S(1)}, u32[]{:S(2)}, u32[]{:S(2)}) %collective-permute-start.31) | collective-permute-done | bytes 786464 | tf_op jit(solution)/shard_map/ppermute | solution.py:46
  522.0 17.4 %collective-permute-done.32 = bf16[384,1024]{1,0:T(8,128)(2,1)S(1)} collective-permute-done((bf16[384,1024]{1,0:T(8,128)(2,1)S(1)}, bf16[384,1024]{1,0:T(8,128)(2,1)S(1)}, u32[]{:S(2)}, u32[]{:S(2)}) %collective-permute-start.32) | collective-permute-done | bytes 786464 | tf_op jit(solution)/shard_map/ppermute | solution.py:46
  (158 shorter events, 101.9 us)
Async XLA Ops:
  6.5 135.3 %all-gather.5.cloned.1.call-start = ((), (), s32[]{:S(2)}) async-start(), calls=%async_computation | async-start | bytes 28311552 | tf_op jit(solution)/shard_map/all_gather | solution.py:267
  11.3 210.2 %all-gather.7.cloned.1.call-start = ((), (), s32[]{:S(2)}) async-start(), calls=%async_computation.1 | async-start | bytes 9437184 | tf_op jit(solution)/shard_map/all_gather | solution.py:268
  12.0 371.1 %all-gather.9.cloned.1.call-start = ((), (), s32[]{:S(2)}) async-start(), calls=%async_computation.2 | async-start | bytes 28311552 | tf_op jit(solution)/shard_map/all_gather | solution.py:269
  16.1 431.9 %all-gather.11.cloned.1.call-start = ((), (), s32[]{:S(2)}) async-start(), calls=%async_computation.3 | async-start | bytes 9437184 | tf_op jit(solution)/shard_map/all_gather | solution.py:270
  17.2 21.2 %collective-permute-start = (bf16[384,1024]{1,0:T(8,128)(2,1)S(1)}, bf16[384,1024]{1,0:T(8,128)(2,1)S(1)}, u32[]{:S(2)}, u32[]{:S(2)}) collective-permute-start(bf16[384,1024]{1,0:T(8,128)(2,1)S(1)} %copy-done.5), channel_id=1, source_target_pairs={{0,1},{1,2},{2,3},{4,5},{5,6},{6,7},{8,9},{9,10},{10,11},{12,13},{... | collective-permute-start | bytes 2359304 | tf_op jit(solution)/shard_map/ppermute | solution.py:22
  20.7 22.3 %collective-permute-start.3 = (bf16[384,1024]{1,0:T(8,128)(2,1)S(1)}, bf16[384,1024]{1,0:T(8,128)(2,1)S(1)}, u32[]{:S(2)}, u32[]{:S(2)}) collective-permute-start(bf16[384,1024]{1,0:T(8,128)(2,1)S(1)} %copy-done.5), channel_id=1, source_target_pairs={{1,0},{2,1},{3,2},{5,4},{6,5},{7,6},{9,8},{10,9},{11,10},{13,12},{... | collective-permute-start | bytes 2359304 | tf_op jit(solution)/shard_map/ppermute | solution.py:23
  38.4 19.5 %collective-permute-start.1 = (bf16[384,1024]{1,0:T(8,128)(2,1)S(1)}, bf16[384,1024]{1,0:T(8,128)(2,1)}, u32[]{:S(2)}, u32[]{:S(2)}) collective-permute-start(bf16[384,1024]{1,0:T(8,128)(2,1)S(1)} %collective-permute-done), channel_id=1, source_target_pairs={{1,2},{2,3},{5,6},{6,7},{9,10},{10,11},{13,14},{14,15},{17,18},{18... | collective-permute-start | bytes 2359304 | tf_op jit(solution)/shard_map/ppermute | solution.py:22
  43.0 21.0 %collective-permute-start.4 = (bf16[384,1024]{1,0:T(8,128)(2,1)S(1)}, bf16[384,1024]{1,0:T(8,128)(2,1)}, u32[]{:S(2)}, u32[]{:S(2)}) collective-permute-start(bf16[384,1024]{1,0:T(8,128)(2,1)S(1)} %collective-permute-done.3), channel_id=1, source_target_pairs={{1,0},{2,1},{5,4},{6,5},{9,8},{10,9},{13,12},{14,13},{17,16},{18,1... | collective-permute-start | bytes 2359304 | tf_op jit(solution)/shard_map/ppermute | solution.py:23
  64.0 17.0 %collective-permute-start.5 = (bf16[384,1024]{1,0:T(8,128)(2,1)}, bf16[384,1024]{1,0:T(8,128)(2,1)S(1)}, u32[]{:S(2)}, u32[]{:S(2)}) collective-permute-start(bf16[384,1024]{1,0:T(8,128)(2,1)} %collective-permute-done.4), channel_id=1, source_target_pairs={{1,0},{5,4},{9,8},{13,12},{17,16},{21,20},{25,24},{29,28}} | collective-permute-start | bytes 2359304 | tf_op jit(solution)/shard_map/ppermute | solution.py:23
  160.2 10.9 %collective-permute-start.6 = (bf16[128,1024]{1,0:T(8,128)(2,1)S(1)}, bf16[128,1024]{1,0:T(8,128)(2,1)S(1)}, u32[]{:S(2)}, u32[]{:S(2)}) collective-permute-start(bf16[128,1024]{1,0:T(8,128)(2,1)S(1)} %get-tuple-element.208), channel_id=1, source_target_pairs={{0,4},{4,8},{8,12},{12,16},{16,20},{20,24},{24,28},{1,5},{5,9},{9,... | collective-permute-start | bytes 786440 | tf_op jit(solution)/shard_map/ppermute | solution.py:142
  231.7 15.2 %collective-permute-start.8 = (bf16[384,1024]{1,0:T(8,128)(2,1)}, bf16[384,1024]{1,0:T(8,128)(2,1)}, u32[]{:S(2)}, u32[]{:S(2)}) collective-permute-start(bf16[384,1024]{1,0:T(8,128)(2,1)} %get-tuple-element.206), channel_id=1, source_target_pairs={{0,1},{4,5},{8,9},{12,13},{16,17},{20,21},{24,25},{28,29}} | collective-permute-start | bytes 2359304 | tf_op jit(solution)/shard_map/ppermute | solution.py:45
  233.0 18.3 %collective-permute-start.11 = (bf16[384,1024]{1,0:T(8,128)(2,1)}, bf16[384,1024]{1,0:T(8,128)(2,1)}, u32[]{:S(2)}, u32[]{:S(2)}) collective-permute-start(bf16[384,1024]{1,0:T(8,128)(2,1)} %get-tuple-element.207), channel_id=1, source_target_pairs={{3,2},{7,6},{11,10},{15,14},{19,18},{23,22},{27,26},{31,30}} | collective-permute-start | bytes 2359304 | tf_op jit(solution)/shard_map/ppermute | solution.py:46
  249.4 14.2 %collective-permute-start.9 = (bf16[384,1024]{1,0:T(8,128)(2,1)}, bf16[384,1024]{1,0:T(8,128)(2,1)}, u32[]{:S(2)}, u32[]{:S(2)}) collective-permute-start(bf16[384,1024]{1,0:T(8,128)(2,1)} %add_convert_fusion.9), channel_id=1, source_target_pairs={{0,1},{1,2},{4,5},{5,6},{8,9},{9,10},{12,13},{13,14},{16,17},{17,1... | collective-permute-start | bytes 2359304 | tf_op jit(solution)/shard_map/ppermute | solution.py:45
  267.4 16.8 %collective-permute-start.12 = (bf16[384,1024]{1,0:T(8,128)(2,1)}, bf16[384,1024]{1,0:T(8,128)(2,1)}, u32[]{:S(2)}, u32[]{:S(2)}) collective-permute-start(bf16[384,1024]{1,0:T(8,128)(2,1)} %get-tuple-element.205), channel_id=1, source_target_pairs={{2,1},{3,2},{6,5},{7,6},{10,9},{11,10},{14,13},{15,14},{18,17},{19... | collective-permute-start | bytes 2359304 | tf_op jit(solution)/shard_map/ppermute | solution.py:46
  268.7 19.8 %collective-permute-start.10 = (bf16[384,1024]{1,0:T(8,128)(2,1)}, bf16[384,1024]{1,0:T(8,128)(2,1)}, u32[]{:S(2)}, u32[]{:S(2)}) collective-permute-start(bf16[384,1024]{1,0:T(8,128)(2,1)} %get-tuple-element.204), channel_id=1, source_target_pairs={{0,1},{1,2},{2,3},{4,5},{5,6},{6,7},{8,9},{9,10},{10,11},{12,13},{... | collective-permute-start | bytes 2359304 | tf_op jit(solution)/shard_map/ppermute | solution.py:45
  286.6 14.2 %collective-permute-start.13 = (bf16[384,1024]{1,0:T(8,128)(2,1)}, bf16[384,1024]{1,0:T(8,128)(2,1)}, u32[]{:S(2)}, u32[]{:S(2)}) collective-permute-start(bf16[384,1024]{1,0:T(8,128)(2,1)} %add_convert_fusion.6), channel_id=1, source_target_pairs={{1,0},{2,1},{3,2},{5,4},{6,5},{7,6},{9,8},{10,9},{11,10},{13,12},{... | collective-permute-start | bytes 2359304 | tf_op jit(solution)/shard_map/ppermute | solution.py:46
  303.9 22.5 %collective-permute-start.14 = (bf16[384,1024]{1,0:T(8,128)(2,1)}, bf16[384,1024]{1,0:T(8,128)(2,1)S(1)}, u32[]{:S(2)}, u32[]{:S(2)}) collective-permute-start(bf16[384,1024]{1,0:T(8,128)(2,1)} %add_convert_fusion.5), channel_id=1, source_target_pairs={{0,1},{1,2},{2,3},{4,5},{5,6},{6,7},{8,9},{9,10},{10,11},{12,13},{... | collective-permute-start | bytes 2359304 | tf_op jit(solution)/shard_map/ppermute | solution.py:22
  322.6 21.2 %collective-permute-start.17 = (bf16[384,1024]{1,0:T(8,128)(2,1)}, bf16[384,1024]{1,0:T(8,128)(2,1)S(1)}, u32[]{:S(2)}, u32[]{:S(2)}) collective-permute-start(bf16[384,1024]{1,0:T(8,128)(2,1)} %add_convert_fusion.5), channel_id=1, source_target_pairs={{1,0},{2,1},{3,2},{5,4},{6,5},{7,6},{9,8},{10,9},{11,10},{13,12},{... | collective-permute-start | bytes 2359304 | tf_op jit(solution)/shard_map/ppermute | solution.py:23
  326.4 21.7 %collective-permute-start.15 = (bf16[384,1024]{1,0:T(8,128)(2,1)S(1)}, bf16[384,1024]{1,0:T(8,128)(2,1)S(1)}, u32[]{:S(2)}, u32[]{:S(2)}) collective-permute-start(bf16[384,1024]{1,0:T(8,128)(2,1)S(1)} %collective-permute-done.14), channel_id=1, source_target_pairs={{1,2},{2,3},{5,6},{6,7},{9,10},{10,11},{13,14},{14,15},{17,18},{18... | collective-permute-start | bytes 2359304 | tf_op jit(solution)/shard_map/ppermute | solution.py:22
  343.8 22.1 %collective-permute-start.18 = (bf16[384,1024]{1,0:T(8,128)(2,1)S(1)}, bf16[384,1024]{1,0:T(8,128)(2,1)S(1)}, u32[]{:S(2)}, u32[]{:S(2)}) collective-permute-start(bf16[384,1024]{1,0:T(8,128)(2,1)S(1)} %collective-permute-done.17), channel_id=1, source_target_pairs={{1,0},{2,1},{5,4},{6,5},{9,8},{10,9},{13,12},{14,13},{17,16},{18,1... | collective-permute-start | bytes 2359304 | tf_op jit(solution)/shard_map/ppermute | solution.py:23
  348.1 22.5 %collective-permute-start.16 = (bf16[384,1024]{1,0:T(8,128)(2,1)S(1)}, bf16[384,1024]{1,0:T(8,128)(2,1)S(1)}, u32[]{:S(2)}, u32[]{:S(2)}) collective-permute-start(bf16[384,1024]{1,0:T(8,128)(2,1)S(1)} %collective-permute-done.15), channel_id=1, source_target_pairs={{2,3},{6,7},{10,11},{14,15},{18,19},{22,23},{26,27},{30,31}} | collective-permute-start | bytes 2359304 | tf_op jit(solution)/shard_map/ppermute | solution.py:22
  366.0 13.9 %collective-permute-start.19 = (bf16[384,1024]{1,0:T(8,128)(2,1)S(1)}, bf16[384,1024]{1,0:T(8,128)(2,1)S(1)}, u32[]{:S(2)}, u32[]{:S(2)}) collective-permute-start(bf16[384,1024]{1,0:T(8,128)(2,1)S(1)} %collective-permute-done.18), channel_id=1, source_target_pairs={{1,0},{5,4},{9,8},{13,12},{17,16},{21,20},{25,24},{29,28}} | collective-permute-start | bytes 2359304 | tf_op jit(solution)/shard_map/ppermute | solution.py:23
  405.6 23.9 %collective-permute-start.20 = (f32[2,16,8,128]{3,2,1,0:T(8,128)S(1)}, f32[2,16,8,128]{3,2,1,0:T(8,128)S(1)}, u32[]{:S(2)}, u32[]{:S(2)}) collective-permute-start(f32[2,16,8,128]{3,2,1,0:T(8,128)S(1)} %block_states.1), channel_id=1, source_target_pairs={{0,4},{4,8},{8,12},{12,16},{16,20},{20,24},{24,28},{28,0},{1,5},{5... | collective-permute-start | bytes 393224 | tf_op jit(solution)/shard_map/ppermute | solution.py:232
  405.7 24.8 %collective-permute-start.21 = (f32[2,16,8,128]{3,2,1,0:T(8,128)S(1)}, f32[2,16,8,128]{3,2,1,0:T(8,128)S(1)}, u32[]{:S(2)}, u32[]{:S(2)}) collective-permute-start(f32[2,16,8,128]{3,2,1,0:T(8,128)S(1)} %block_states.1), channel_id=1, source_target_pairs={{0,8},{4,12},{8,16},{12,20},{16,24},{20,28},{24,0},{28,4},{1,9},{5... | collective-permute-start | bytes 393224 | tf_op jit(solution)/shard_map/ppermute | solution.py:232
  405.7 27.1 %collective-permute-start.22 = (f32[2,16,8,128]{3,2,1,0:T(8,128)S(1)}, f32[2,16,8,128]{3,2,1,0:T(8,128)S(1)}, u32[]{:S(2)}, u32[]{:S(2)}) collective-permute-start(f32[2,16,8,128]{3,2,1,0:T(8,128)S(1)} %block_states.1), channel_id=1, source_target_pairs={{0,12},{4,16},{8,20},{12,24},{16,28},{20,0},{24,4},{28,8},{1,13},{... | collective-permute-start | bytes 393224 | tf_op jit(solution)/shard_map/ppermute | solution.py:232
  428.0 11.7 %collective-permute-start.24 = (f32[2,16,8,128]{3,2,1,0:T(8,128)S(1)}, f32[2,16,8,128]{3,2,1,0:T(8,128)S(1)}, u32[]{:S(2)}, u32[]{:S(2)}) collective-permute-start(f32[2,16,8,128]{3,2,1,0:T(8,128)S(1)} %block_states.1), channel_id=1, source_target_pairs={{0,20},{4,24},{8,28},{12,0},{16,4},{20,8},{24,12},{28,16},{1,21},{... | collective-permute-start | bytes 393224 | tf_op jit(solution)/shard_map/ppermute | solution.py:232
  455.3 22.0 %collective-permute-start.27 = (bf16[384,1024]{1,0:T(8,128)(2,1)S(1)}, bf16[384,1024]{1,0:T(8,128)(2,1)S(1)}, u32[]{:S(2)}, u32[]{:S(2)}) collective-permute-start(bf16[384,1024]{1,0:T(8,128)(2,1)S(1)} %get-tuple-element.202), channel_id=1, source_target_pairs={{0,1},{4,5},{8,9},{12,13},{16,17},{20,21},{24,25},{28,29}} | collective-permute-start | bytes 2359304 | tf_op jit(solution)/shard_map/ppermute | solution.py:45
  456.6 23.0 %collective-permute-start.30 = (bf16[384,1024]{1,0:T(8,128)(2,1)S(1)}, bf16[384,1024]{1,0:T(8,128)(2,1)S(1)}, u32[]{:S(2)}, u32[]{:S(2)}) collective-permute-start(bf16[384,1024]{1,0:T(8,128)(2,1)S(1)} %get-tuple-element.203), channel_id=1, source_target_pairs={{3,2},{7,6},{11,10},{15,14},{19,18},{23,22},{27,26},{31,30}} | collective-permute-start | bytes 2359304 | tf_op jit(solution)/shard_map/ppermute | solution.py:46
  477.6 21.2 %collective-permute-start.28 = (bf16[384,1024]{1,0:T(8,128)(2,1)S(1)}, bf16[384,1024]{1,0:T(8,128)(2,1)S(1)}, u32[]{:S(2)}, u32[]{:S(2)}) collective-permute-start(bf16[384,1024]{1,0:T(8,128)(2,1)S(1)} %add_convert_fusion.4), channel_id=1, source_target_pairs={{0,1},{1,2},{4,5},{5,6},{8,9},{9,10},{12,13},{13,14},{16,17},{17,1... | collective-permute-start | bytes 2359304 | tf_op jit(solution)/shard_map/ppermute | solution.py:45
  499.5 20.3 %collective-permute-start.31 = (bf16[384,1024]{1,0:T(8,128)(2,1)S(1)}, bf16[384,1024]{1,0:T(8,128)(2,1)S(1)}, u32[]{:S(2)}, u32[]{:S(2)}) collective-permute-start(bf16[384,1024]{1,0:T(8,128)(2,1)S(1)} %get-tuple-element.201), channel_id=1, source_target_pairs={{2,1},{3,2},{6,5},{7,6},{10,9},{11,10},{14,13},{15,14},{18,17},{19... | collective-permute-start | bytes 2359304 | tf_op jit(solution)/shard_map/ppermute | solution.py:46
  500.8 21.2 %collective-permute-start.29 = (bf16[384,1024]{1,0:T(8,128)(2,1)S(1)}, bf16[384,1024]{1,0:T(8,128)(2,1)S(1)}, u32[]{:S(2)}, u32[]{:S(2)}) collective-permute-start(bf16[384,1024]{1,0:T(8,128)(2,1)S(1)} %get-tuple-element.200), channel_id=1, source_target_pairs={{0,1},{1,2},{2,3},{4,5},{5,6},{6,7},{8,9},{9,10},{10,11},{12,13},{... | collective-permute-start | bytes 2359304 | tf_op jit(solution)/shard_map/ppermute | solution.py:45
  520.1 19.4 %collective-permute-start.32 = (bf16[384,1024]{1,0:T(8,128)(2,1)S(1)}, bf16[384,1024]{1,0:T(8,128)(2,1)S(1)}, u32[]{:S(2)}, u32[]{:S(2)}) collective-permute-start(bf16[384,1024]{1,0:T(8,128)(2,1)S(1)} %add_convert_fusion.1), channel_id=1, source_target_pairs={{1,0},{2,1},{3,2},{5,4},{6,5},{7,6},{9,8},{10,9},{11,10},{13,12},{... | collective-permute-start | bytes 2359304 | tf_op jit(solution)/shard_map/ppermute | solution.py:46
  (18 other events, 348.7 us)
Sparse Core Ops, SparseCore 0:
  11.4 130.4 all-gather.4
  143.7 57.1 all-gather.6
  202.8 130.2 all-gather.8
  334.8 56.0 all-gather.10
where the time goes:
time: 551 us; the launch traced here: 549 us
  waiting for transfers between devices  266 us (48%)
  starting transfers between devices  89.1 us (16%)
  Pallas kernels  63 us (11%)
  matrix products  45.7 us (8%)
  local copies, waits for them, and re-layouts  39.3 us (7%)
  between operations  24.3 us (4%)
  other arithmetic  21.7 us (4%)
    ppermute x6, waiting for transfers between devices, scatter_channels(): right = lax.ppermute(rightward.astype(jnp.bfloat16), 'ch', up)  63.6 us
    all_gather x1, waiting for transfers between devices, body(): mr_in = lax.all_gather(mr_inproj, 'ctx', axis=0, tiled=True)  57.3 us
    ppermute x6, waiting for transfers between devices, scatter_channels(): left = lax.ppermute(leftward.astype(jnp.bfloat16), 'ch', down)  55.1 us
    pallas_call x1, Pallas kernels, short_mix(): pl.pallas_call(short_kernel, out_shape=jax.ShapeDtypeStruct((2, span_rows...  50.1 us
    ppermute x6, waiting for transfers between devices, gather_channels(): from_right.append(lax.ppermute(from_right[-1], 'ch', down))  45.4 us
    dot_general x2, matrix products, features_in(): jnp.dot(normed, flat, preferred_element_type=jnp.float32)  31.3 us
    ppermute x6, waiting for transfers between devices, gather_channels(): from_left.append(lax.ppermute(from_left[-1], 'ch', up))  28.3 us
    ppermute x7, starting transfers between devices, long_mix(): states = lax.ppermute(finals, 'ctx', ring)  27.2 us
  transfers between devices with their start and end apart: 37, of which 19 were waited for; matrix products, arithmetic and copies ran while one was open for 15% of the time, Pallas kernels for 11%

commit v1 on v0

--- a/solution.py
+++ b/solution.py
@@ -25,32 +25,41 @@
     return lax.dynamic_slice_in_dim(line, (count - 1 - index) * channels, count * channels, 1)
 
 
-def scatter_channels(terms, stream):
+def scatter_channels(terms, streams):
     count, index = (lax.axis_size("ch"), lax.axis_index("ch"))
-    channels = stream.shape[1]
-
-    def block(number):
+    rows, channels = streams[0].shape
+    parts = range(len(streams))
+
+    def block(part, number):
         begin = jnp.clip(number, 0, count - 1) * channels
-        return lax.dynamic_slice_in_dim(terms, begin, channels, 1).astype(jnp.float32)
-
-    total = block(index) + stream.astype(jnp.float32)
-    right, left = (None, None)
+        own = terms[part * rows : (part + 1) * rows]
+        return lax.dynamic_slice_in_dim(own, begin, channels, 1).astype(jnp.float32)
+
+    right, left = ([None for _ in parts], [None for _ in parts])
     for far in range(count - 1, 0, -1):
         up = [(i, i + 1) for i in range(count - far)]
         down = [(i, i - 1) for i in range(far, count)]
-        rightward, leftward = (block(index + far), block(index - far))
-        if right is not None:
-            rightward = rightward + right.astype(jnp.float32)
-            leftward = leftward + left.astype(jnp.float32)
-        right = lax.ppermute(rightward.astype(jnp.bfloat16), "ch", up)
-        left = lax.ppermute(leftward.astype(jnp.bfloat16), "ch", down)
-    return (total + right.astype(jnp.float32) + left.astype(jnp.float32)).astype(jnp.bfloat16)
-
-
-def features_in(stream, gain, piece):
-    whole = gather_channels(stream)
+        for part in parts:
+            rightward, leftward = (block(part, index + far), block(part, index - far))
+            if right[part] is not None:
+                rightward = rightward + right[part].astype(jnp.float32)
+                leftward = leftward + left[part].astype(jnp.float32)
+            right[part] = lax.ppermute(rightward.astype(jnp.bfloat16), "ch", up)
+            left[part] = lax.ppermute(leftward.astype(jnp.bfloat16), "ch", down)
+    summed = []
+    for part in parts:
+        total = block(part, index) + streams[part].astype(jnp.float32)
+        total = total + right[part].astype(jnp.float32) + left[part].astype(jnp.float32)
+        summed.append(total.astype(jnp.bfloat16))
+    return summed
+
+
+def features_in(streams, gain, piece, early):
+    whole = jnp.concatenate([gather_channels(part) for part in streams], axis=0)
     floats = whole.astype(jnp.float32)
     scaled = lax.rsqrt(jnp.mean(floats * floats, axis=1, keepdims=True) + 1e-06)
+    if early is not None:
+        scaled, early = lax.optimization_barrier((scaled, early))
     normed = (floats * scaled * gain[None, :]).astype(jnp.bfloat16)
     channels = piece.shape[2]
     flat = piece.reshape(piece.shape[0], 3 * channels)
@@ -59,13 +68,13 @@
         joined[:, channels : 2 * channels].astype(jnp.float32)
         * joined[:, 2 * channels :].astype(jnp.float32)
     ).astype(jnp.bfloat16)
-    return (joined[:, :channels], product)
-
-
-def features_out(stream, query, mixed, piece):
+    return (joined[:, :channels], product, early)
+
+
+def features_out(streams, query, mixed, piece):
     gated = (query.astype(jnp.float32) * mixed).astype(jnp.bfloat16)
     terms = jnp.dot(gated, piece, preferred_element_type=jnp.float32).astype(jnp.bfloat16)
-    return scatter_channels(terms, stream)
+    return scatter_channels(terms, streams)
 
 
 def span_layout(shard_rows):
@@ -197,18 +206,33 @@
         lax.fori_loop(0, span_rows, step, tuple(initial[half, m] for m in range(modes)))
 
 
-def long_mix(product, li_decay, li_residue, doc_ids):
-    shard_rows, channels = product.shape
+def long_tables(shard_rows, li_decay, li_residue, doc_ids):
     ctx_count, ctx_index, span_rows, span_starts = span_layout(shard_rows)
-    modes = li_decay.shape[0]
+    modes, channels = li_decay.shape
     tile = (channels // LANES, LANES)
-    values = product.astype(jnp.float32).reshape((2, span_rows) + tile)
     decay = li_decay.reshape((modes,) + tile)
     residue = li_residue.reshape((modes,) + tile)
     factor = jnp.exp(-decay)
     places = span_starts[:, None] + jnp.arange(span_rows)[None, :]
     earlier = jnp.take(doc_ids, jnp.clip(places - 1, 0, None))
     follows = ((places > 0) & (jnp.take(doc_ids, places) == earlier)).astype(jnp.float32)
+    source = (ctx_index - jnp.arange(ctx_count)) % ctx_count
+    block = jnp.stack([source, 2 * ctx_count - 1 - source], 1)
+    last = (block + 1) * span_rows - 1
+    gap = span_starts - 1 - last[:, :, None]
+    keep = (gap >= 0) & (jnp.take(doc_ids, last)[:, :, None] == earlier[:, 0])
+    distance = jnp.where(keep, gap, 0).astype(jnp.float32)[..., None, None, None]
+    weights = jnp.exp(-decay * distance) * keep.astype(jnp.float32)[..., None, None, None]
+    return (factor, residue, follows, weights)
+
+
+def long_mix(product, tables):
+    shard_rows, channels = product.shape
+    ctx_count, ctx_index, span_rows, span_starts = span_layout(shard_rows)
+    factor, residue, follows, weights = tables
+    modes = factor.shape[0]
+    tile = (channels // LANES, LANES)
+    values = product.astype(jnp.float32).reshape((2, span_rows) + tile)
     params = pltpu.CompilerParams(vmem_limit_bytes=VMEM_LIMIT)
     flops = 2 * shard_rows * modes * channels
     finals = pl.pallas_call(
@@ -222,21 +246,14 @@
         ),
         name="block_states",
     )(follows, factor, values)
-    before_docs = earlier[:, 0]
     initial = jnp.zeros((2, modes) + tile, jnp.float32)
     for shift in range(ctx_count):
-        source = (ctx_index - shift) % ctx_count
         states = finals
         if shift:
             ring = [(i, (i + shift) % ctx_count) for i in range(ctx_count)]
             states = lax.ppermute(finals, "ctx", ring)
-        for part, block in enumerate((source, 2 * ctx_count - 1 - source)):
-            last = (block + 1) * span_rows - 1
-            gap = span_starts - 1 - last
-            keep = (gap >= 0) & (jnp.take(doc_ids, last) == before_docs)
-            distance = jnp.where(keep, gap, 0).astype(jnp.float32)[:, None, None, None]
-            weight = jnp.exp(-decay[None] * distance) * keep.astype(jnp.float32)[:, None, None, None]
-            initial = initial + weight * states[part][None]
+        for part in range(2):
+            initial = initial + weights[shift, part] * states[part][None]
     mixed = pl.pallas_call(
         long_kernel,
         out_shape=jax.ShapeDtypeStruct((2, span_rows) + tile, jnp.float32),
@@ -268,10 +285,14 @@
     mr_out = lax.all_gather(mr_outproj, "ctx", axis=1, tiled=True)
     li_in = lax.all_gather(li_inproj, "ctx", axis=0, tiled=True)
     li_out = lax.all_gather(li_outproj, "ctx", axis=1, tiled=True)
-    query, product = features_in(tokens, mr_gain, mr_in)
-    stream = features_out(tokens, query, short_mix(product, mr_filter, doc_ids), mr_out)
-    query, product = features_in(stream, li_gain, li_in)
-    return features_out(stream, query, long_mix(product, li_decay, li_residue, doc_ids), li_out)
+    shard_rows = tokens.shape[0]
+    early = long_tables(shard_rows, li_decay, li_residue, doc_ids)
+    streams = [tokens[: shard_rows // 2], tokens[shard_rows // 2 :]]
+    query, product, tables = features_in([tokens], mr_gain, mr_in, early)
+    streams = features_out(streams, query, short_mix(product, mr_filter, doc_ids), mr_out)
+    query, product, _ = features_in(streams, li_gain, li_in, None)
+    streams = features_out(streams, query, long_mix(product, tables), li_out)
+    return jnp.concatenate(streams, axis=0)
 
 
 def solution(mesh):

time: 551 us -> 493 us (0.89)
  waiting for transfers between devices: 266 us -> 178 us
  starting transfers between devices: 89.1 us -> 129 us
  between operations: 24.3 us -> 14.4 us
    ppermute x12 -> x24, waiting for transfers between devices: 119 us -> 74.3 us  [the longest x12 46.1 us: scatter_channels(): right[part] = lax.ppermute(rightward.astype(jnp.bfloat16), 'ch', up)]
    ppermute x6 -> x9, waiting for transfers between devices: 45.4 us -> 15.6 us  [gather_channels(): from_right.append(lax.ppermute(from_right[-1], 'ch', down))]
    ppermute x12 -> x24, starting transfers between devices: 24.3 us -> 47.8 us  [the longest x12 28.2 us: scatter_channels(): right[part] = lax.ppermute(rightward.astype(jnp.bfloat16), 'ch', up)]
    ppermute x6 -> x9, starting transfers between devices: 18.4 us -> 31.3 us  [gather_channels(): from_right.append(lax.ppermute(from_right[-1], 'ch', down))]
    ppermute x6 -> x9, waiting for transfers between devices: 28.3 us -> 17.3 us  [gather_channels(): from_left.append(lax.ppermute(from_left[-1], 'ch', up))]
    unnamed x47 -> x57, local copies, waits for them, and re-layouts: 26.5 us -> 21.2 us
    ppermute x6 -> x9, starting transfers between devices: 14.5 us -> 18 us  [gather_channels(): from_left.append(lax.ppermute(from_left[-1], 'ch', up))]
    convert_element_type x13 -> x18, other arithmetic: 15.8 us -> 16.6 us  [the longest x8 9.54 us: scatter_channels(): right[part] = lax.ppermute(rightward.astype(jnp.bfloat16), 'ch', up)]
  transfers between devices with their start and end apart: 37 -> 55, of which waited for: 19 -> 28; matrix products, arithmetic and copies ran while one was open for 15% -> 18% of each run, Pallas kernels for 11% -> 13%
where the time goes in v1:
time: 493 us; the launch traced here: 490 us
  waiting for transfers between devices  178 us (36%)
  starting transfers between devices  129 us (26%)
  Pallas kernels  63 us (13%)
  matrix products  44.3 us (9%)
  local copies, waits for them, and re-layouts  36.9 us (7%)
  other arithmetic  24.4 us (5%)
  between operations  14.4 us (3%)
    all_gather x1, waiting for transfers between devices, body(): mr_in = lax.all_gather(mr_inproj, 'ctx', axis=0, tiled=True)  57.3 us
    pallas_call x1, Pallas kernels, short_mix(): pl.pallas_call(short_kernel, out_shape=jax.ShapeDtypeStruct((2, span_rows...  50.1 us
    ppermute x12, waiting for transfers between devices, scatter_channels(): right[part] = lax.ppermute(rightward.astype(jnp.bfloat16), 'ch', up)  46.1 us
    ppermute x9, starting transfers between devices, gather_channels(): from_right.append(lax.ppermute(from_right[-1], 'ch', down))  31.3 us
    dot_general x2, matrix products, features_in(): jnp.dot(normed, flat, preferred_element_type=jnp.float32)  29.9 us
    ppermute x12, waiting for transfers between devices, scatter_channels(): left[part] = lax.ppermute(leftward.astype(jnp.bfloat16), 'ch', down)  28.2 us
    ppermute x12, starting transfers between devices, scatter_channels(): right[part] = lax.ppermute(rightward.astype(jnp.bfloat16), 'ch', up)  28.2 us
    ppermute x7, starting transfers between devices, long_mix(): states = lax.ppermute(finals, 'ctx', ring)  27.4 us
  transfers between devices with their start and end apart: 55, of which 28 were waited for; matrix products, arithmetic and copies ran while one was open for 18% of the time, Pallas kernels for 13%

profile of v1, /device:TPU:14, one launch (start us, length us, event | category | flops | bytes accessed | tf_op | source)
XLA Modules:
  0.0 489.7 jit_solution(9662193386245443928)
XLA Ops:
  6.5 4.8 copy.18
  34.1 4.3 collective-permute-done
  38.5 4.4 collective-permute-start.1
  45.0 12.9 %collective-permute-done.1 = bf16[384,1024]{1,0:T(8,128)(2,1)} collective-permute-done((bf16[384,1024]{1,0:T(8,128)(2,1)S(1)}, bf16[384,1024]{1,0:T(8,128)(2,1)}, u32[]{:S(2)}, u32[]{:S(2)}) %collective-permute-start.1) | collective-permute-done | bytes 786464 | tf_op jit(solution)/shard_map/ppermute | solution.py:22
  75.0 5.9 %collective-permute-done.5 = bf16[384,1024]{1,0:T(8,128)(2,1)S(1)} collective-permute-done((bf16[384,1024]{1,0:T(8,128)(2,1)}, bf16[384,1024]{1,0:T(8,128)(2,1)S(1)}, u32[]{:S(2)}, u32[]{:S(2)}) %collective-permute-start.5) | collective-permute-done | bytes 786464 | tf_op jit(solution)/shard_map/ppermute | solution.py:23
  84.6 57.3 %all-gather.5.cloned.1.call-done = bf16[4096,3,1024]{0,2,1:T(8,128)(2,1)} async-done(((bf16[512,3,1024]{0,2,1:T(8,128)(2,1)}), bf16[4096,3,1024]{0,2,1:T(8,128)(2,1)}) %all-gather.5.cloned.1.call-update) | async-done | bytes 25165840 | tf_op jit(solution)/shard_map/all_gather | solution.py:284
  141.9 15.7 %convolution_convert_fusion.3 = bf16[384,3072]{1,0:T(8,128)(2,1)S(1)} fusion(bf16[4096,3072]{0,1:T(8,128)(2,1)} %bitcast.201, f32[4096]{0:T(1024)S(1)} %copy-done.13, f32[384]{0:T(512)S(1)} %reduce.1, bf16[384,7168]{1,0:T(8,128)(2,1)} %constant_dynamic-update-slice_fusion, s32[]{:T(128)S(6)} %select_n.138), kind=kOutput, calls=%fused_computation.17 | convolution fusion | flops 9671147520 | bytes 30688772 | tf_op jit(solution)/shard_map/dot_general | solution.py:66
  163.0 4.4 collective-permute-done.7
  171.4 50.1 %short_mix.1 = f32[2,192,8,128]{3,2,1,0:T(8,128)S(1)} custom-call(s32[2,320]{1,0:T(2,128)S(1)} %compare_select_fusion.3.docs, f32[2,320,8,128]{3,2,1,0:T(8,128)S(1)} %maximum_convert_fusion.window, f32[143,8,128]{2,1,0:T(8,128)S(1)} %slice.253.taps), custom_call_target="tpu_custom_call" | custom-call | flops 100663296 | bytes 3145728 | tf_op jit(solution)/shard_map/short_mix/pallas_call | solution.py:161
  221.5 7.3 %convolution_convert_fusion.1 = bf16[384,4096]{1,0:T(8,128)(2,1)S(1)} fusion(bf16[1024,4096]{1,0:T(8,128)(2,1)} %all-gather.7.cloned.1.call-done, f32[48,8,8,128]{3,2,1,0:T(8,128)S(1)} %bitcast.188, bf16[384,3072]{1,0:T(8,128)(2,1)} %copy-done.3), kind=kOutput, calls=%fused_computation.15 | convolution fusion | flops 3223977984 | bytes 13893632 | tf_op jit(solution)/shard_map/dot_general | solution.py:76
  234.9 8.4 %collective-permute-done.20 = bf16[192,1024]{1,0:T(8,128)(2,1)} collective-permute-done((bf16[192,1024]{1,0:T(8,128)(2,1)}, bf16[192,1024]{1,0:T(8,128)(2,1)}, u32[]{:S(2)}, u32[]{:S(2)}) %collective-permute-start.20) | collective-permute-done | bytes 393248 | tf_op jit(solution)/shard_map/ppermute | solution.py:47
  259.9 5.0 %collective-permute-done.9 = bf16[192,1024]{1,0:T(8,128)(2,1)} collective-permute-done((bf16[192,1024]{1,0:T(8,128)(2,1)}, bf16[192,1024]{1,0:T(8,128)(2,1)}, u32[]{:S(2)}, u32[]{:S(2)}) %collective-permute-start.9) | collective-permute-done | bytes 393248 | tf_op jit(solution)/shard_map/ppermute | solution.py:47
  268.6 4.6 collective-permute-start.22
  277.4 4.2 collective-permute-start.25
  285.5 4.3 collective-permute-done.25
  289.8 8.4 %collective-permute-done.13 = bf16[192,1024]{1,0:T(8,128)(2,1)} collective-permute-done((bf16[192,1024]{1,0:T(8,128)(2,1)}, bf16[192,1024]{1,0:T(8,128)(2,1)}, u32[]{:S(2)}, u32[]{:S(2)}) %collective-permute-start.13) | collective-permute-done | bytes 393248 | tf_op jit(solution)/shard_map/ppermute | solution.py:48
  315.8 4.4 collective-permute-start.18
  324.3 4.4 collective-permute-start.30
  329.7 4.4 collective-permute-start.19
  344.7 14.3 %convolution_convert_fusion.2 = bf16[384,3072]{1,0:T(8,128)(2,1)S(1)} fusion(bf16[4096,3072]{0,1:T(8,128)(2,1)} %bitcast.200, f32[4096]{0:T(1024)S(1)} %copy-done.14, f32[384]{0:T(512)S(1)} %add_rsqrt_fusion, bf16[192,4096]{1,0:T(8,128)(2,1)S(1)} %constant_dynamic-slice_fusion.4, bf16[192,4096]{1,0:T(8,128)(2,1)S(1)} %constant_dynamic-slice_fusion.7), kind=kOutput, calls=%fused_computation.16 | convolution fusion | flops 9675866112 | bytes 30688768 | tf_op jit(solution)/shard_map/dot_general | solution.py:66
  360.3 5.4 %block_states.1 = f32[2,16,8,128]{3,2,1,0:T(8,128)S(1)} custom-call(f32[2,192]{1,0:T(2,128)S(1)} %and_convert_fusion.follows, f32[16,8,128]{2,1,0:T(8,128)S(1)} %bitcast_exponential_fusion.factor, f32[2,192,8,128]{3,2,1,0:T(8,128)S(1)} %bitcast.185), custom_call_target="tpu_custom_call" | custom-call | flops 12582912 | bytes 1572864 | tf_op jit(solution)/shard_map/block_states/pallas_call | solution.py:238
  368.9 14.3 %collective-permute-start.34 = (f32[2,16,8,128]{3,2,1,0:T(8,128)S(1)}, f32[2,16,8,128]{3,2,1,0:T(8,128)S(1)}, u32[]{:S(2)}, u32[]{:S(2)}) collective-permute-start(f32[2,16,8,128]{3,2,1,0:T(8,128)S(1)} %block_states.1), channel_id=1, source_target_pairs={{0,12},{4,16},{8,20},{12,24},{16,28},{20,0},{24,4},{28,8},{1,13},{... | collective-permute-start | bytes 393224 | tf_op jit(solution)/shard_map/ppermute | solution.py:254
  388.3 4.8 collective-permute-start.38
  397.7 7.5 %long_mix.1 = f32[2,192,8,128]{3,2,1,0:T(8,128)S(1)} custom-call(f32[2,192]{1,0:T(2,128)S(1)} %and_convert_fusion.follows, f32[16,8,128]{2,1,0:T(8,128)S(1)} %bitcast_exponential_fusion.factor, f32[16,8,128]{2,1,0:T(8,128)S(1)} %bitcast.189, f32[2,16,8,128]{3,2,1,0:T(8,128)S(1)} %fusion.19.initial, f32[2,192,8,128]{3,2,1,0:T(8,128)S(1)} %bitcast.186), custom_call_target="tpu_custom_call" | custom-call | flops 25165824 | bytes 3145728 | tf_op jit(solution)/shard_map/long_mix/pallas_call | solution.py:257
  405.3 7.1 %convolution_convert_fusion = bf16[384,4096]{1,0:T(8,128)(2,1)S(1)} fusion(bf16[1024,4096]{1,0:T(8,128)(2,1)} %all-gather.11.cloned.1.call-done, f32[48,8,8,128]{3,2,1,0:T(8,128)S(1)} %bitcast.187, bf16[384,3072]{1,0:T(8,128)(2,1)} %copy-done.10), kind=kOutput, calls=%fused_computation.14 | convolution fusion | flops 3223977984 | bytes 13893632 | tf_op jit(solution)/shard_map/dot_general | solution.py:76
  416.1 10.5 %collective-permute-done.39 = bf16[192,1024]{1,0:T(8,128)(2,1)S(1)} collective-permute-done((bf16[192,1024]{1,0:T(8,128)(2,1)S(1)}, bf16[192,1024]{1,0:T(8,128)(2,1)S(1)}, u32[]{:S(2)}, u32[]{:S(2)}) %collective-permute-start.39) | collective-permute-done | bytes 393248 | tf_op jit(solution)/shard_map/ppermute | solution.py:47
  429.4 5.7 %collective-permute-done.45 = bf16[192,1024]{1,0:T(8,128)(2,1)S(1)} collective-permute-done((bf16[192,1024]{1,0:T(8,128)(2,1)S(1)}, bf16[192,1024]{1,0:T(8,128)(2,1)S(1)}, u32[]{:S(2)}, u32[]{:S(2)}) %collective-permute-start.45) | collective-permute-done | bytes 393248 | tf_op jit(solution)/shard_map/ppermute | solution.py:47
  437.1 6.3 %collective-permute-done.40 = bf16[192,1024]{1,0:T(8,128)(2,1)S(1)} collective-permute-done((bf16[192,1024]{1,0:T(8,128)(2,1)S(1)}, bf16[192,1024]{1,0:T(8,128)(2,1)S(1)}, u32[]{:S(2)}, u32[]{:S(2)}) %collective-permute-start.40) | collective-permute-done | bytes 393248 | tf_op jit(solution)/shard_map/ppermute | solution.py:47
  445.3 6.5 %collective-permute-done.46 = bf16[192,1024]{1,0:T(8,128)(2,1)S(1)} collective-permute-done((bf16[192,1024]{1,0:T(8,128)(2,1)S(1)}, bf16[192,1024]{1,0:T(8,128)(2,1)S(1)}, u32[]{:S(2)}, u32[]{:S(2)}) %collective-permute-start.46) | collective-permute-done | bytes 393248 | tf_op jit(solution)/shard_map/ppermute | solution.py:47
  453.5 4.6 collective-permute-start.41
  468.2 6.3 %collective-permute-done.44 = bf16[192,1024]{1,0:T(8,128)(2,1)S(1)} collective-permute-done((bf16[192,1024]{1,0:T(8,128)(2,1)S(1)}, bf16[192,1024]{1,0:T(8,128)(2,1)S(1)}, u32[]{:S(2)}, u32[]{:S(2)}) %collective-permute-start.44) | collective-permute-done | bytes 393248 | tf_op jit(solution)/shard_map/ppermute | solution.py:48
  474.8 7.1 %collective-permute-done.50 = bf16[192,1024]{1,0:T(8,128)(2,1)S(1)} collective-permute-done((bf16[192,1024]{1,0:T(8,128)(2,1)S(1)}, bf16[192,1024]{1,0:T(8,128)(2,1)S(1)}, u32[]{:S(2)}, u32[]{:S(2)}) %collective-permute-start.50) | collective-permute-done | bytes 393248 | tf_op jit(solution)/shard_map/ppermute | solution.py:48
  (231 shorter events, 159.9 us)
Async XLA Ops:
  6.5 135.4 %all-gather.5.cloned.1.call-start = ((), (), s32[]{:S(2)}) async-start(), calls=%async_computation | async-start | bytes 28311552 | tf_op jit(solution)/shard_map/all_gather | solution.py:284
  11.3 210.2 %all-gather.7.cloned.1.call-start = ((), (), s32[]{:S(2)}) async-start(), calls=%async_computation.1 | async-start | bytes 9437184 | tf_op jit(solution)/shard_map/all_gather | solution.py:285
  12.1 332.6 %all-gather.9.cloned.1.call-start = ((), (), s32[]{:S(2)}) async-start(), calls=%async_computation.2 | async-start | bytes 28311552 | tf_op jit(solution)/shard_map/all_gather | solution.py:286
  16.2 389.1 %all-gather.11.cloned.1.call-start = ((), (), s32[]{:S(2)}) async-start(), calls=%async_computation.3 | async-start | bytes 9437184 | tf_op jit(solution)/shard_map/all_gather | solution.py:287
  17.3 21.2 %collective-permute-start = (bf16[384,1024]{1,0:T(8,128)(2,1)S(1)}, bf16[384,1024]{1,0:T(8,128)(2,1)S(1)}, u32[]{:S(2)}, u32[]{:S(2)}) collective-permute-start(bf16[384,1024]{1,0:T(8,128)(2,1)S(1)} %copy-done.9), channel_id=1, source_target_pairs={{0,1},{1,2},{2,3},{4,5},{5,6},{6,7},{8,9},{9,10},{10,11},{12,13},{... | collective-permute-start | bytes 2359304 | tf_op jit(solution)/shard_map/ppermute | solution.py:22
  20.8 22.3 %collective-permute-start.3 = (bf16[384,1024]{1,0:T(8,128)(2,1)S(1)}, bf16[384,1024]{1,0:T(8,128)(2,1)S(1)}, u32[]{:S(2)}, u32[]{:S(2)}) collective-permute-start(bf16[384,1024]{1,0:T(8,128)(2,1)S(1)} %copy-done.9), channel_id=1, source_target_pairs={{1,0},{2,1},{3,2},{5,4},{6,5},{7,6},{9,8},{10,9},{11,10},{13,12},{... | collective-permute-start | bytes 2359304 | tf_op jit(solution)/shard_map/ppermute | solution.py:23
  38.5 19.5 %collective-permute-start.1 = (bf16[384,1024]{1,0:T(8,128)(2,1)S(1)}, bf16[384,1024]{1,0:T(8,128)(2,1)}, u32[]{:S(2)}, u32[]{:S(2)}) collective-permute-start(bf16[384,1024]{1,0:T(8,128)(2,1)S(1)} %collective-permute-done), channel_id=1, source_target_pairs={{1,2},{2,3},{5,6},{6,7},{9,10},{10,11},{13,14},{14,15},{17,18},{18... | collective-permute-start | bytes 2359304 | tf_op jit(solution)/shard_map/ppermute | solution.py:22
  43.1 20.2 %collective-permute-start.4 = (bf16[384,1024]{1,0:T(8,128)(2,1)S(1)}, bf16[384,1024]{1,0:T(8,128)(2,1)}, u32[]{:S(2)}, u32[]{:S(2)}) collective-permute-start(bf16[384,1024]{1,0:T(8,128)(2,1)S(1)} %collective-permute-done.3), channel_id=1, source_target_pairs={{1,0},{2,1},{5,4},{6,5},{9,8},{10,9},{13,12},{14,13},{17,16},{18,1... | collective-permute-start | bytes 2359304 | tf_op jit(solution)/shard_map/ppermute | solution.py:23
  63.3 17.6 %collective-permute-start.5 = (bf16[384,1024]{1,0:T(8,128)(2,1)}, bf16[384,1024]{1,0:T(8,128)(2,1)S(1)}, u32[]{:S(2)}, u32[]{:S(2)}) collective-permute-start(bf16[384,1024]{1,0:T(8,128)(2,1)} %collective-permute-done.4), channel_id=1, source_target_pairs={{1,0},{5,4},{9,8},{13,12},{17,16},{21,20},{25,24},{29,28}} | collective-permute-start | bytes 2359304 | tf_op jit(solution)/shard_map/ppermute | solution.py:23
  232.2 16.6 %collective-permute-start.8 = (bf16[192,1024]{1,0:T(8,128)(2,1)}, bf16[192,1024]{1,0:T(8,128)(2,1)}, u32[]{:S(2)}, u32[]{:S(2)}) collective-permute-start(bf16[192,1024]{1,0:T(8,128)(2,1)} %get-tuple-element.32), channel_id=1, source_target_pairs={{0,1},{4,5},{8,9},{12,13},{16,17},{20,21},{24,25},{28,29}} | collective-permute-start | bytes 1179656 | tf_op jit(solution)/shard_map/ppermute | solution.py:47
  233.5 19.1 %collective-permute-start.23 = (bf16[192,1024]{1,0:T(8,128)(2,1)}, bf16[192,1024]{1,0:T(8,128)(2,1)}, u32[]{:S(2)}, u32[]{:S(2)}) collective-permute-start(bf16[192,1024]{1,0:T(8,128)(2,1)} %get-tuple-element.37), channel_id=1, source_target_pairs={{3,2},{7,6},{11,10},{15,14},{19,18},{23,22},{27,26},{31,30}} | collective-permute-start | bytes 1179656 | tf_op jit(solution)/shard_map/ppermute | solution.py:48
  250.6 14.3 %collective-permute-start.9 = (bf16[192,1024]{1,0:T(8,128)(2,1)}, bf16[192,1024]{1,0:T(8,128)(2,1)}, u32[]{:S(2)}, u32[]{:S(2)}) collective-permute-start(bf16[192,1024]{1,0:T(8,128)(2,1)} %add_convert_fusion.19), channel_id=1, source_target_pairs={{0,1},{1,2},{4,5},{5,6},{8,9},{9,10},{12,13},{13,14},{16,17},{17,1... | collective-permute-start | bytes 1179656 | tf_op jit(solution)/shard_map/ppermute | solution.py:47
  258.6 16.9 %collective-permute-start.24 = (bf16[192,1024]{1,0:T(8,128)(2,1)}, bf16[192,1024]{1,0:T(8,128)(2,1)}, u32[]{:S(2)}, u32[]{:S(2)}) collective-permute-start(bf16[192,1024]{1,0:T(8,128)(2,1)} %get-tuple-element.35), channel_id=1, source_target_pairs={{2,1},{3,2},{6,5},{7,6},{10,9},{11,10},{14,13},{15,14},{18,17},{19... | collective-permute-start | bytes 1179656 | tf_op jit(solution)/shard_map/ppermute | solution.py:48
  267.3 14.4 %collective-permute-start.12 = (bf16[192,1024]{1,0:T(8,128)(2,1)}, bf16[192,1024]{1,0:T(8,128)(2,1)}, u32[]{:S(2)}, u32[]{:S(2)}) collective-permute-start(bf16[192,1024]{1,0:T(8,128)(2,1)} %get-tuple-element.31), channel_id=1, source_target_pairs={{2,1},{3,2},{6,5},{7,6},{10,9},{11,10},{14,13},{15,14},{18,17},{19... | collective-permute-start | bytes 1179656 | tf_op jit(solution)/shard_map/ppermute | solution.py:48
  268.6 16.9 %collective-permute-start.22 = (bf16[192,1024]{1,0:T(8,128)(2,1)}, bf16[192,1024]{1,0:T(8,128)(2,1)}, u32[]{:S(2)}, u32[]{:S(2)}) collective-permute-start(bf16[192,1024]{1,0:T(8,128)(2,1)} %get-tuple-element.34), channel_id=1, source_target_pairs={{0,1},{1,2},{2,3},{4,5},{5,6},{6,7},{8,9},{9,10},{10,11},{12,13},{... | collective-permute-start | bytes 1179656 | tf_op jit(solution)/shard_map/ppermute | solution.py:47
  283.6 14.6 %collective-permute-start.13 = (bf16[192,1024]{1,0:T(8,128)(2,1)}, bf16[192,1024]{1,0:T(8,128)(2,1)}, u32[]{:S(2)}, u32[]{:S(2)}) collective-permute-start(bf16[192,1024]{1,0:T(8,128)(2,1)} %add_convert_fusion.16), channel_id=1, source_target_pairs={{1,0},{2,1},{3,2},{5,4},{6,5},{7,6},{9,8},{10,9},{11,10},{13,12},{... | collective-permute-start | bytes 1179656 | tf_op jit(solution)/shard_map/ppermute | solution.py:48
  308.2 16.0 %collective-permute-start.29 = (bf16[192,1024]{1,0:T(8,128)(2,1)S(1)}, bf16[192,1024]{1,0:T(8,128)(2,1)S(1)}, u32[]{:S(2)}, u32[]{:S(2)}) collective-permute-start(bf16[192,1024]{1,0:T(8,128)(2,1)S(1)} %get-tuple-element.39), channel_id=1, source_target_pairs={{1,0},{2,1},{3,2},{5,4},{6,5},{7,6},{9,8},{10,9},{11,10},{13,12},{... | collective-permute-start | bytes 1179656 | tf_op jit(solution)/shard_map/ppermute | solution.py:23
  312.2 16.5 %collective-permute-start.15 = (bf16[192,1024]{1,0:T(8,128)(2,1)S(1)}, bf16[192,1024]{1,0:T(8,128)(2,1)S(1)}, u32[]{:S(2)}, u32[]{:S(2)}) collective-permute-start(bf16[192,1024]{1,0:T(8,128)(2,1)S(1)} %collective-permute-done.14), channel_id=1, source_target_pairs={{1,2},{2,3},{5,6},{6,7},{9,10},{10,11},{13,14},{14,15},{17,18},{18... | collective-permute-start | bytes 1179656 | tf_op jit(solution)/shard_map/ppermute | solution.py:22
  365.7 18.9 %collective-permute-start.32 = (f32[2,16,8,128]{3,2,1,0:T(8,128)S(1)}, f32[2,16,8,128]{3,2,1,0:T(8,128)S(1)}, u32[]{:S(2)}, u32[]{:S(2)}) collective-permute-start(f32[2,16,8,128]{3,2,1,0:T(8,128)S(1)} %block_states.1), channel_id=1, source_target_pairs={{0,4},{4,8},{8,12},{12,16},{16,20},{20,24},{24,28},{28,0},{1,5},{5... | collective-permute-start | bytes 393224 | tf_op jit(solution)/shard_map/ppermute | solution.py:254
  365.8 22.6 %collective-permute-start.33 = (f32[2,16,8,128]{3,2,1,0:T(8,128)S(1)}, f32[2,16,8,128]{3,2,1,0:T(8,128)S(1)}, u32[]{:S(2)}, u32[]{:S(2)}) collective-permute-start(f32[2,16,8,128]{3,2,1,0:T(8,128)S(1)} %block_states.1), channel_id=1, source_target_pairs={{0,8},{4,12},{8,16},{12,20},{16,24},{20,28},{24,0},{28,4},{1,9},{5... | collective-permute-start | bytes 393224 | tf_op jit(solution)/shard_map/ppermute | solution.py:254
  368.9 24.3 %collective-permute-start.34 = (f32[2,16,8,128]{3,2,1,0:T(8,128)S(1)}, f32[2,16,8,128]{3,2,1,0:T(8,128)S(1)}, u32[]{:S(2)}, u32[]{:S(2)}) collective-permute-start(f32[2,16,8,128]{3,2,1,0:T(8,128)S(1)} %block_states.1), channel_id=1, source_target_pairs={{0,12},{4,16},{8,20},{12,24},{16,28},{20,0},{24,4},{28,8},{1,13},{... | collective-permute-start | bytes 393224 | tf_op jit(solution)/shard_map/ppermute | solution.py:254
  414.1 20.9 %collective-permute-start.45 = (bf16[192,1024]{1,0:T(8,128)(2,1)S(1)}, bf16[192,1024]{1,0:T(8,128)(2,1)S(1)}, u32[]{:S(2)}, u32[]{:S(2)}) collective-permute-start(bf16[192,1024]{1,0:T(8,128)(2,1)S(1)} %get-tuple-element.28), channel_id=1, source_target_pairs={{0,1},{4,5},{8,9},{12,13},{16,17},{20,21},{24,25},{28,29}} | collective-permute-start | bytes 1179656 | tf_op jit(solution)/shard_map/ppermute | solution.py:47
  415.4 21.7 %collective-permute-start.42 = (bf16[192,1024]{1,0:T(8,128)(2,1)S(1)}, bf16[192,1024]{1,0:T(8,128)(2,1)S(1)}, u32[]{:S(2)}, u32[]{:S(2)}) collective-permute-start(bf16[192,1024]{1,0:T(8,128)(2,1)S(1)} %get-tuple-element.25), channel_id=1, source_target_pairs={{3,2},{7,6},{11,10},{15,14},{19,18},{23,22},{27,26},{31,30}} | collective-permute-start | bytes 1179656 | tf_op jit(solution)/shard_map/ppermute | solution.py:48
  426.8 16.7 %collective-permute-start.40 = (bf16[192,1024]{1,0:T(8,128)(2,1)S(1)}, bf16[192,1024]{1,0:T(8,128)(2,1)S(1)}, u32[]{:S(2)}, u32[]{:S(2)}) collective-permute-start(bf16[192,1024]{1,0:T(8,128)(2,1)S(1)} %add_convert_fusion.9), channel_id=1, source_target_pairs={{0,1},{1,2},{4,5},{5,6},{8,9},{9,10},{12,13},{13,14},{16,17},{17,1... | collective-permute-start | bytes 1179656 | tf_op jit(solution)/shard_map/ppermute | solution.py:47
  428.7 16.5 %collective-permute-start.48 = (bf16[192,1024]{1,0:T(8,128)(2,1)S(1)}, bf16[192,1024]{1,0:T(8,128)(2,1)S(1)}, u32[]{:S(2)}, u32[]{:S(2)}) collective-permute-start(bf16[192,1024]{1,0:T(8,128)(2,1)S(1)} %get-tuple-element.29), channel_id=1, source_target_pairs={{3,2},{7,6},{11,10},{15,14},{19,18},{23,22},{27,26},{31,30}} | collective-permute-start | bytes 1179656 | tf_op jit(solution)/shard_map/ppermute | solution.py:48
  435.2 16.6 %collective-permute-start.46 = (bf16[192,1024]{1,0:T(8,128)(2,1)S(1)}, bf16[192,1024]{1,0:T(8,128)(2,1)S(1)}, u32[]{:S(2)}, u32[]{:S(2)}) collective-permute-start(bf16[192,1024]{1,0:T(8,128)(2,1)S(1)} %add_convert_fusion.4), channel_id=1, source_target_pairs={{0,1},{1,2},{4,5},{5,6},{8,9},{9,10},{12,13},{13,14},{16,17},{17,1... | collective-permute-start | bytes 1179656 | tf_op jit(solution)/shard_map/ppermute | solution.py:47
  443.8 14.3 %collective-permute-start.43 = (bf16[192,1024]{1,0:T(8,128)(2,1)S(1)}, bf16[192,1024]{1,0:T(8,128)(2,1)S(1)}, u32[]{:S(2)}, u32[]{:S(2)}) collective-permute-start(bf16[192,1024]{1,0:T(8,128)(2,1)S(1)} %get-tuple-element.23), channel_id=1, source_target_pairs={{2,1},{3,2},{6,5},{7,6},{10,9},{11,10},{14,13},{15,14},{18,17},{19... | collective-permute-start | bytes 1179656 | tf_op jit(solution)/shard_map/ppermute | solution.py:48
  452.1 14.0 %collective-permute-start.49 = (bf16[192,1024]{1,0:T(8,128)(2,1)S(1)}, bf16[192,1024]{1,0:T(8,128)(2,1)S(1)}, u32[]{:S(2)}, u32[]{:S(2)}) collective-permute-start(bf16[192,1024]{1,0:T(8,128)(2,1)S(1)} %get-tuple-element.27), channel_id=1, source_target_pairs={{2,1},{3,2},{6,5},{7,6},{10,9},{11,10},{14,13},{15,14},{18,17},{19... | collective-permute-start | bytes 1179656 | tf_op jit(solution)/shard_map/ppermute | solution.py:48
  453.5 14.7 %collective-permute-start.41 = (bf16[192,1024]{1,0:T(8,128)(2,1)S(1)}, bf16[192,1024]{1,0:T(8,128)(2,1)S(1)}, u32[]{:S(2)}, u32[]{:S(2)}) collective-permute-start(bf16[192,1024]{1,0:T(8,128)(2,1)S(1)} %get-tuple-element.22), channel_id=1, source_target_pairs={{0,1},{1,2},{2,3},{4,5},{5,6},{6,7},{8,9},{9,10},{10,11},{12,13},{... | collective-permute-start | bytes 1179656 | tf_op jit(solution)/shard_map/ppermute | solution.py:47
  458.2 16.3 %collective-permute-start.44 = (bf16[192,1024]{1,0:T(8,128)(2,1)S(1)}, bf16[192,1024]{1,0:T(8,128)(2,1)S(1)}, u32[]{:S(2)}, u32[]{:S(2)}) collective-permute-start(bf16[192,1024]{1,0:T(8,128)(2,1)S(1)} %add_convert_fusion.6), channel_id=1, source_target_pairs={{1,0},{2,1},{3,2},{5,4},{6,5},{7,6},{9,8},{10,9},{11,10},{13,12},{... | collective-permute-start | bytes 1179656 | tf_op jit(solution)/shard_map/ppermute | solution.py:48
  460.2 14.7 %collective-permute-start.47 = (bf16[192,1024]{1,0:T(8,128)(2,1)S(1)}, bf16[192,1024]{1,0:T(8,128)(2,1)S(1)}, u32[]{:S(2)}, u32[]{:S(2)}) collective-permute-start(bf16[192,1024]{1,0:T(8,128)(2,1)S(1)} %get-tuple-element.26), channel_id=1, source_target_pairs={{0,1},{1,2},{2,3},{4,5},{5,6},{6,7},{8,9},{9,10},{10,11},{12,13},{... | collective-permute-start | bytes 1179656 | tf_op jit(solution)/shard_map/ppermute | solution.py:47
  466.3 15.7 %collective-permute-start.50 = (bf16[192,1024]{1,0:T(8,128)(2,1)S(1)}, bf16[192,1024]{1,0:T(8,128)(2,1)S(1)}, u32[]{:S(2)}, u32[]{:S(2)}) collective-permute-start(bf16[192,1024]{1,0:T(8,128)(2,1)S(1)} %add_convert_fusion.1), channel_id=1, source_target_pairs={{1,0},{2,1},{3,2},{5,4},{6,5},{7,6},{9,8},{10,9},{11,10},{13,12},{... | collective-permute-start | bytes 1179656 | tf_op jit(solution)/shard_map/ppermute | solution.py:48
  (38 other events, 591.9 us)
Sparse Core Ops, SparseCore 0:
  11.4 130.4 all-gather.4
  143.8 57.1 all-gather.6
  202.8 130.2 all-gather.8
  334.9 63.0 all-gather.10

commit v2 on v1

--- a/solution.py
+++ b/solution.py
@@ -1,3 +1,5 @@
+import functools
+
 import jax
 import jax.numpy as jnp
 from jax import lax
@@ -96,7 +98,7 @@
         first_doc = docs[half, reach + row]
         last_doc = docs[half, reach + row + ROWS - 1]
 
-        def sources(step, sums):
+        def sources(whole, step, sums):
             begin = row + step * ROWS
             base = reach - step * ROWS
 
@@ -123,15 +125,18 @@
                         sums[a] = sums[a] + (source[b] * same) * weight[a - b + ROWS - 1]
                 return tuple(sums)
 
-            return lax.cond(docs[half, begin] == last_doc, plain, masked, sums)
-
-        def outside(step, skipped):
-            return skipped + jnp.where(docs[half, row + step * ROWS + ROWS - 1] < first_doc, 1, 0)
+            return plain(sums) if whole else masked(sums)
+
+        def outside(step, counts):
+            begin = row + step * ROWS
+            skipped = counts[0] + jnp.where(docs[half, begin + ROWS - 1] < first_doc, 1, 0)
+            return skipped, counts[1] + jnp.where(docs[half, begin] == last_doc, 0, 1)
 
         steps = reach // ROWS + 1
-        skip = lax.fori_loop(0, steps, outside, jnp.int32(0))
-        zero = jnp.zeros(tile, jnp.float32)
-        sums = lax.fori_loop(skip, steps, sources, (zero,) * ROWS)
+        skip, mixed = lax.fori_loop(0, steps, outside, (jnp.int32(0), jnp.int32(0)))
+        sums = (jnp.zeros(tile, jnp.float32),) * ROWS
+        sums = lax.fori_loop(skip, mixed, functools.partial(sources, False), sums)
+        sums = lax.fori_loop(mixed, steps, functools.partial(sources, True), sums)
         for a in range(ROWS):
             out[half, row + a] = sums[a]
         return 0

time: 493 us -> 488 us (0.990)
  Pallas kernels: 63 us -> 46.7 us
  waiting for transfers between devices: 178 us -> 192 us
    pallas_call x1, Pallas kernels: 50.1 us -> 33.8 us  [short_mix(): pl.pallas_call(short_kernel, out_shape=jax.ShapeDtypeStruct((2, span_rows...]
    ppermute x7, waiting for transfers between devices: 4.17 us -> 11 us  [long_mix(): states = lax.ppermute(finals, 'ctx', ring)]
    ppermute x7, starting transfers between devices: 27.4 us -> 20.8 us  [long_mix(): states = lax.ppermute(finals, 'ctx', ring)]
    all_gather x1, waiting for transfers between devices: 0.02 us -> 6.59 us  [body(): li_out = lax.all_gather(li_outproj, 'ctx', axis=1, tiled=True)]
  transfers between devices with their start and end apart: 55 -> 55, of which waited for: 28 -> 31; matrix products, arithmetic and copies ran while one was open for 18% -> 18% of each run, Pallas kernels for 13% -> 10%
where the time goes in v2:
time: 488 us; the launch traced here: 485 us
  waiting for transfers between devices  192 us (39%)
  starting transfers between devices  127 us (26%)
  Pallas kernels  46.7 us (10%)
  matrix products  44.4 us (9%)
  local copies, waits for them, and re-layouts  36.9 us (8%)
  other arithmetic  24.1 us (5%)
  between operations  14.3 us (3%)
    all_gather x1, waiting for transfers between devices, body(): mr_in = lax.all_gather(mr_inproj, 'ctx', axis=0, tiled=True)  57.3 us
    ppermute x12, waiting for transfers between devices, scatter_channels(): right[part] = lax.ppermute(rightward.astype(jnp.bfloat16), 'ch', up)  45.4 us
    pallas_call x1, Pallas kernels, short_mix(): pl.pallas_call(short_kernel, out_shape=jax.ShapeDtypeStruct((2, span_rows...  33.8 us
    ppermute x9, starting transfers between devices, gather_channels(): from_right.append(lax.ppermute(from_right[-1], 'ch', down))  31.3 us
    ppermute x12, starting transfers between devices, scatter_channels(): right[part] = lax.ppermute(rightward.astype(jnp.bfloat16), 'ch', up)  30.5 us
    dot_general x2, matrix products, features_in(): jnp.dot(normed, flat, preferred_element_type=jnp.float32)  30.2 us
    ppermute x12, waiting for transfers between devices, scatter_channels(): left[part] = lax.ppermute(leftward.astype(jnp.bfloat16), 'ch', down)  26 us
    ppermute x9, starting transfers between devices, gather_channels(): from_left.append(lax.ppermute(from_left[-1], 'ch', up))  22.4 us
  transfers between devices with their start and end apart: 55, of which 31 were waited for; matrix products, arithmetic and copies ran while one was open for 18% of the time, Pallas kernels for 10%

profile of v2, /device:TPU:14, one launch (start us, length us, event | category | flops | bytes accessed | tf_op | source)
XLA Modules:
  0.0 485.4 jit_solution(7240938837463725382)
XLA Ops:
  6.5 4.8 copy.18
  34.1 4.3 collective-permute-done
  38.5 4.4 collective-permute-start.1
  45.0 12.9 %collective-permute-done.1 = bf16[384,1024]{1,0:T(8,128)(2,1)} collective-permute-done((bf16[384,1024]{1,0:T(8,128)(2,1)S(1)}, bf16[384,1024]{1,0:T(8,128)(2,1)}, u32[]{:S(2)}, u32[]{:S(2)}) %collective-permute-start.1) | collective-permute-done | bytes 786464 | tf_op jit(solution)/shard_map/ppermute | solution.py:24
  75.0 5.9 %collective-permute-done.5 = bf16[384,1024]{1,0:T(8,128)(2,1)S(1)} collective-permute-done((bf16[384,1024]{1,0:T(8,128)(2,1)}, bf16[384,1024]{1,0:T(8,128)(2,1)S(1)}, u32[]{:S(2)}, u32[]{:S(2)}) %collective-permute-start.5) | collective-permute-done | bytes 786464 | tf_op jit(solution)/shard_map/ppermute | solution.py:25
  84.6 57.3 %all-gather.5.cloned.1.call-done = bf16[4096,3,1024]{0,2,1:T(8,128)(2,1)} async-done(((bf16[512,3,1024]{0,2,1:T(8,128)(2,1)}), bf16[4096,3,1024]{0,2,1:T(8,128)(2,1)}) %all-gather.5.cloned.1.call-update) | async-done | bytes 25165840 | tf_op jit(solution)/shard_map/all_gather | solution.py:289
  141.9 15.7 %convolution_convert_fusion.3 = bf16[384,3072]{1,0:T(8,128)(2,1)S(1)} fusion(bf16[4096,3072]{0,1:T(8,128)(2,1)} %bitcast.201, f32[4096]{0:T(1024)S(1)} %copy-done.13, f32[384]{0:T(512)S(1)} %reduce.1, bf16[384,7168]{1,0:T(8,128)(2,1)} %constant_dynamic-update-slice_fusion, s32[]{:T(128)S(6)} %select_n.138), kind=kOutput, calls=%fused_computation.17 | convolution fusion | flops 9671147520 | bytes 30688772 | tf_op jit(solution)/shard_map/dot_general | solution.py:68
  163.0 4.4 collective-permute-done.7
  171.4 33.8 %short_mix.1 = f32[2,192,8,128]{3,2,1,0:T(8,128)S(1)} custom-call(s32[2,320]{1,0:T(2,128)S(1)} %compare_select_fusion.3.docs, f32[2,320,8,128]{3,2,1,0:T(8,128)S(1)} %maximum_convert_fusion.window, f32[143,8,128]{2,1,0:T(8,128)S(1)} %slice.253.taps), custom_call_target="tpu_custom_call" | custom-call | flops 100663296 | bytes 3145728 | tf_op jit(solution)/shard_map/short_mix/pallas_call | solution.py:166
  205.2 7.1 %convolution_convert_fusion.1 = bf16[384,4096]{1,0:T(8,128)(2,1)S(1)} fusion(bf16[1024,4096]{1,0:T(8,128)(2,1)} %all-gather.7.cloned.1.call-done, f32[48,8,8,128]{3,2,1,0:T(8,128)S(1)} %bitcast.188, bf16[384,3072]{1,0:T(8,128)(2,1)} %copy-done.3), kind=kOutput, calls=%fused_computation.15 | convolution fusion | flops 3223977984 | bytes 13893632 | tf_op jit(solution)/shard_map/dot_general | solution.py:78
  218.4 9.3 %collective-permute-done.20 = bf16[192,1024]{1,0:T(8,128)(2,1)} collective-permute-done((bf16[192,1024]{1,0:T(8,128)(2,1)}, bf16[192,1024]{1,0:T(8,128)(2,1)}, u32[]{:S(2)}, u32[]{:S(2)}) %collective-permute-start.20) | collective-permute-done | bytes 393248 | tf_op jit(solution)/shard_map/ppermute | solution.py:49
  251.6 4.6 collective-permute-start.22
  256.2 4.7 collective-permute-start.10
  270.0 5.4 %collective-permute-done.25 = bf16[192,1024]{1,0:T(8,128)(2,1)} collective-permute-done((bf16[192,1024]{1,0:T(8,128)(2,1)}, bf16[192,1024]{1,0:T(8,128)(2,1)}, u32[]{:S(2)}, u32[]{:S(2)}) %collective-permute-start.25) | collective-permute-done | bytes 393248 | tf_op jit(solution)/shard_map/ppermute | solution.py:50
  301.7 4.4 collective-permute-start.27
  314.1 4.4 collective-permute-start.19
  322.5 4.6 collective-permute-start.31
  334.5 14.6 %convolution_convert_fusion.2 = bf16[384,3072]{1,0:T(8,128)(2,1)S(1)} fusion(bf16[4096,3072]{0,1:T(8,128)(2,1)} %bitcast.200, f32[4096]{0:T(1024)S(1)} %copy-done.14, f32[384]{0:T(512)S(1)} %add_rsqrt_fusion, bf16[192,4096]{1,0:T(8,128)(2,1)S(1)} %constant_dynamic-slice_fusion.4, bf16[192,4096]{1,0:T(8,128)(2,1)S(1)} %constant_dynamic-slice_fusion.7), kind=kOutput, calls=%fused_computation.16 | convolution fusion | flops 9675866112 | bytes 30688768 | tf_op jit(solution)/shard_map/dot_general | solution.py:68
  350.5 5.4 %block_states.1 = f32[2,16,8,128]{3,2,1,0:T(8,128)S(1)} custom-call(f32[2,192]{1,0:T(2,128)S(1)} %and_convert_fusion.follows, f32[16,8,128]{2,1,0:T(8,128)S(1)} %bitcast_exponential_fusion.factor, f32[2,192,8,128]{3,2,1,0:T(8,128)S(1)} %bitcast.185), custom_call_target="tpu_custom_call" | custom-call | flops 12582912 | bytes 1572864 | tf_op jit(solution)/shard_map/block_states/pallas_call | solution.py:243
  355.9 8.6 %collective-permute-start.33 = (f32[2,16,8,128]{3,2,1,0:T(8,128)S(1)}, f32[2,16,8,128]{3,2,1,0:T(8,128)S(1)}, u32[]{:S(2)}, u32[]{:S(2)}) collective-permute-start(f32[2,16,8,128]{3,2,1,0:T(8,128)S(1)} %block_states.1), channel_id=1, source_target_pairs={{0,8},{4,12},{8,16},{12,20},{16,24},{20,28},{24,0},{28,4},{1,9},{5... | collective-permute-start | bytes 393224 | tf_op jit(solution)/shard_map/ppermute | solution.py:259
  371.6 5.1 %collective-permute-start.38 = (f32[2,16,8,128]{3,2,1,0:T(8,128)S(1)}, f32[2,16,8,128]{3,2,1,0:T(8,128)S(1)}, u32[]{:S(2)}, u32[]{:S(2)}) collective-permute-start(f32[2,16,8,128]{3,2,1,0:T(8,128)S(1)} %block_states.1), channel_id=1, source_target_pairs={{0,28},{4,0},{8,4},{12,8},{16,12},{20,16},{24,20},{28,24},{1,29},{... | collective-permute-start | bytes 393224 | tf_op jit(solution)/shard_map/ppermute | solution.py:259
  376.8 7.4 %collective-permute-done.36 = f32[2,16,8,128]{3,2,1,0:T(8,128)S(1)} collective-permute-done((f32[2,16,8,128]{3,2,1,0:T(8,128)S(1)}, f32[2,16,8,128]{3,2,1,0:T(8,128)S(1)}, u32[]{:S(2)}, u32[]{:S(2)}) %collective-permute-start.36) | collective-permute-done | bytes 131104 | tf_op jit(solution)/shard_map/ppermute | solution.py:259
  388.0 7.5 %long_mix.1 = f32[2,192,8,128]{3,2,1,0:T(8,128)S(1)} custom-call(f32[2,192]{1,0:T(2,128)S(1)} %and_convert_fusion.follows, f32[16,8,128]{2,1,0:T(8,128)S(1)} %bitcast_exponential_fusion.factor, f32[16,8,128]{2,1,0:T(8,128)S(1)} %bitcast.189, f32[2,16,8,128]{3,2,1,0:T(8,128)S(1)} %fusion.19.initial, f32[2,192,8,128]{3,2,1,0:T(8,128)S(1)} %bitcast.186), custom_call_target="tpu_custom_call" | custom-call | flops 25165824 | bytes 3145728 | tf_op jit(solution)/shard_map/long_mix/pallas_call | solution.py:262
  395.5 6.6 %all-gather.11.cloned.1.call-done = bf16[1024,4096]{1,0:T(8,128)(2,1)} async-done(((bf16[1024,512]{1,0:T(8,128)(2,1)}), bf16[1024,4096]{1,0:T(8,128)(2,1)}) %all-gather.11.cloned.1.call-update) | async-done | bytes 8388624 | tf_op jit(solution)/shard_map/all_gather | solution.py:292
  402.1 7.1 %convolution_convert_fusion = bf16[384,4096]{1,0:T(8,128)(2,1)S(1)} fusion(bf16[1024,4096]{1,0:T(8,128)(2,1)} %all-gather.11.cloned.1.call-done, f32[48,8,8,128]{3,2,1,0:T(8,128)S(1)} %bitcast.187, bf16[384,3072]{1,0:T(8,128)(2,1)} %copy-done.10), kind=kOutput, calls=%fused_computation.14 | convolution fusion | flops 3223977984 | bytes 13893632 | tf_op jit(solution)/shard_map/dot_general | solution.py:78
  412.9 10.5 %collective-permute-done.39 = bf16[192,1024]{1,0:T(8,128)(2,1)S(1)} collective-permute-done((bf16[192,1024]{1,0:T(8,128)(2,1)S(1)}, bf16[192,1024]{1,0:T(8,128)(2,1)S(1)}, u32[]{:S(2)}, u32[]{:S(2)}) %collective-permute-start.39) | collective-permute-done | bytes 393248 | tf_op jit(solution)/shard_map/ppermute | solution.py:49
  426.2 5.7 %collective-permute-done.45 = bf16[192,1024]{1,0:T(8,128)(2,1)S(1)} collective-permute-done((bf16[192,1024]{1,0:T(8,128)(2,1)S(1)}, bf16[192,1024]{1,0:T(8,128)(2,1)S(1)}, u32[]{:S(2)}, u32[]{:S(2)}) %collective-permute-start.45) | collective-permute-done | bytes 393248 | tf_op jit(solution)/shard_map/ppermute | solution.py:49
  433.9 6.3 %collective-permute-done.40 = bf16[192,1024]{1,0:T(8,128)(2,1)S(1)} collective-permute-done((bf16[192,1024]{1,0:T(8,128)(2,1)S(1)}, bf16[192,1024]{1,0:T(8,128)(2,1)S(1)}, u32[]{:S(2)}, u32[]{:S(2)}) %collective-permute-start.40) | collective-permute-done | bytes 393248 | tf_op jit(solution)/shard_map/ppermute | solution.py:49
  442.0 6.0 %collective-permute-done.46 = bf16[192,1024]{1,0:T(8,128)(2,1)S(1)} collective-permute-done((bf16[192,1024]{1,0:T(8,128)(2,1)S(1)}, bf16[192,1024]{1,0:T(8,128)(2,1)S(1)}, u32[]{:S(2)}, u32[]{:S(2)}) %collective-permute-start.46) | collective-permute-done | bytes 393248 | tf_op jit(solution)/shard_map/ppermute | solution.py:49
  449.8 4.6 collective-permute-start.41
  464.5 6.3 %collective-permute-done.44 = bf16[192,1024]{1,0:T(8,128)(2,1)S(1)} collective-permute-done((bf16[192,1024]{1,0:T(8,128)(2,1)S(1)}, bf16[192,1024]{1,0:T(8,128)(2,1)S(1)}, u32[]{:S(2)}, u32[]{:S(2)}) %collective-permute-start.44) | collective-permute-done | bytes 393248 | tf_op jit(solution)/shard_map/ppermute | solution.py:50
  471.1 6.6 %collective-permute-done.50 = bf16[192,1024]{1,0:T(8,128)(2,1)S(1)} collective-permute-done((bf16[192,1024]{1,0:T(8,128)(2,1)S(1)}, bf16[192,1024]{1,0:T(8,128)(2,1)S(1)}, u32[]{:S(2)}, u32[]{:S(2)}) %collective-permute-start.50) | collective-permute-done | bytes 393248 | tf_op jit(solution)/shard_map/ppermute | solution.py:50
  (231 shorter events, 175.2 us)
Async XLA Ops:
  6.5 135.4 %all-gather.5.cloned.1.call-start = ((), (), s32[]{:S(2)}) async-start(), calls=%async_computation | async-start | bytes 28311552 | tf_op jit(solution)/shard_map/all_gather | solution.py:289
  11.3 193.9 %all-gather.7.cloned.1.call-start = ((), (), s32[]{:S(2)}) async-start(), calls=%async_computation.1 | async-start | bytes 9437184 | tf_op jit(solution)/shard_map/all_gather | solution.py:290
  12.1 322.4 %all-gather.9.cloned.1.call-start = ((), (), s32[]{:S(2)}) async-start(), calls=%async_computation.2 | async-start | bytes 28311552 | tf_op jit(solution)/shard_map/all_gather | solution.py:291
  16.2 385.9 %all-gather.11.cloned.1.call-start = ((), (), s32[]{:S(2)}) async-start(), calls=%async_computation.3 | async-start | bytes 9437184 | tf_op jit(solution)/shard_map/all_gather | solution.py:292
  17.3 21.2 %collective-permute-start = (bf16[384,1024]{1,0:T(8,128)(2,1)S(1)}, bf16[384,1024]{1,0:T(8,128)(2,1)S(1)}, u32[]{:S(2)}, u32[]{:S(2)}) collective-permute-start(bf16[384,1024]{1,0:T(8,128)(2,1)S(1)} %copy-done.9), channel_id=1, source_target_pairs={{0,1},{1,2},{2,3},{4,5},{5,6},{6,7},{8,9},{9,10},{10,11},{12,13},{... | collective-permute-start | bytes 2359304 | tf_op jit(solution)/shard_map/ppermute | solution.py:24
  20.8 22.3 %collective-permute-start.3 = (bf16[384,1024]{1,0:T(8,128)(2,1)S(1)}, bf16[384,1024]{1,0:T(8,128)(2,1)S(1)}, u32[]{:S(2)}, u32[]{:S(2)}) collective-permute-start(bf16[384,1024]{1,0:T(8,128)(2,1)S(1)} %copy-done.9), channel_id=1, source_target_pairs={{1,0},{2,1},{3,2},{5,4},{6,5},{7,6},{9,8},{10,9},{11,10},{13,12},{... | collective-permute-start | bytes 2359304 | tf_op jit(solution)/shard_map/ppermute | solution.py:25
  38.5 19.5 %collective-permute-start.1 = (bf16[384,1024]{1,0:T(8,128)(2,1)S(1)}, bf16[384,1024]{1,0:T(8,128)(2,1)}, u32[]{:S(2)}, u32[]{:S(2)}) collective-permute-start(bf16[384,1024]{1,0:T(8,128)(2,1)S(1)} %collective-permute-done), channel_id=1, source_target_pairs={{1,2},{2,3},{5,6},{6,7},{9,10},{10,11},{13,14},{14,15},{17,18},{18... | collective-permute-start | bytes 2359304 | tf_op jit(solution)/shard_map/ppermute | solution.py:24
  43.1 20.2 %collective-permute-start.4 = (bf16[384,1024]{1,0:T(8,128)(2,1)S(1)}, bf16[384,1024]{1,0:T(8,128)(2,1)}, u32[]{:S(2)}, u32[]{:S(2)}) collective-permute-start(bf16[384,1024]{1,0:T(8,128)(2,1)S(1)} %collective-permute-done.3), channel_id=1, source_target_pairs={{1,0},{2,1},{5,4},{6,5},{9,8},{10,9},{13,12},{14,13},{17,16},{18,1... | collective-permute-start | bytes 2359304 | tf_op jit(solution)/shard_map/ppermute | solution.py:25
  63.3 17.6 %collective-permute-start.5 = (bf16[384,1024]{1,0:T(8,128)(2,1)}, bf16[384,1024]{1,0:T(8,128)(2,1)S(1)}, u32[]{:S(2)}, u32[]{:S(2)}) collective-permute-start(bf16[384,1024]{1,0:T(8,128)(2,1)} %collective-permute-done.4), channel_id=1, source_target_pairs={{1,0},{5,4},{9,8},{13,12},{17,16},{21,20},{25,24},{29,28}} | collective-permute-start | bytes 2359304 | tf_op jit(solution)/shard_map/ppermute | solution.py:25
  215.7 20.4 %collective-permute-start.8 = (bf16[192,1024]{1,0:T(8,128)(2,1)}, bf16[192,1024]{1,0:T(8,128)(2,1)}, u32[]{:S(2)}, u32[]{:S(2)}) collective-permute-start(bf16[192,1024]{1,0:T(8,128)(2,1)} %get-tuple-element.32), channel_id=1, source_target_pairs={{0,1},{4,5},{8,9},{12,13},{16,17},{20,21},{24,25},{28,29}} | collective-permute-start | bytes 1179656 | tf_op jit(solution)/shard_map/ppermute | solution.py:49
  217.0 22.9 %collective-permute-start.23 = (bf16[192,1024]{1,0:T(8,128)(2,1)}, bf16[192,1024]{1,0:T(8,128)(2,1)}, u32[]{:S(2)}, u32[]{:S(2)}) collective-permute-start(bf16[192,1024]{1,0:T(8,128)(2,1)} %get-tuple-element.37), channel_id=1, source_target_pairs={{3,2},{7,6},{11,10},{15,14},{19,18},{23,22},{27,26},{31,30}} | collective-permute-start | bytes 1179656 | tf_op jit(solution)/shard_map/ppermute | solution.py:50
  231.5 15.8 %collective-permute-start.11 = (bf16[192,1024]{1,0:T(8,128)(2,1)}, bf16[192,1024]{1,0:T(8,128)(2,1)}, u32[]{:S(2)}, u32[]{:S(2)}) collective-permute-start(bf16[192,1024]{1,0:T(8,128)(2,1)} %get-tuple-element.33), channel_id=1, source_target_pairs={{3,2},{7,6},{11,10},{15,14},{19,18},{23,22},{27,26},{31,30}} | collective-permute-start | bytes 1179656 | tf_op jit(solution)/shard_map/ppermute | solution.py:50
  250.3 15.8 %collective-permute-start.12 = (bf16[192,1024]{1,0:T(8,128)(2,1)}, bf16[192,1024]{1,0:T(8,128)(2,1)}, u32[]{:S(2)}, u32[]{:S(2)}) collective-permute-start(bf16[192,1024]{1,0:T(8,128)(2,1)} %get-tuple-element.31), channel_id=1, source_target_pairs={{2,1},{3,2},{6,5},{7,6},{10,9},{11,10},{14,13},{15,14},{18,17},{19... | collective-permute-start | bytes 1179656 | tf_op jit(solution)/shard_map/ppermute | solution.py:50
  251.6 18.4 %collective-permute-start.22 = (bf16[192,1024]{1,0:T(8,128)(2,1)}, bf16[192,1024]{1,0:T(8,128)(2,1)}, u32[]{:S(2)}, u32[]{:S(2)}) collective-permute-start(bf16[192,1024]{1,0:T(8,128)(2,1)} %get-tuple-element.34), channel_id=1, source_target_pairs={{0,1},{1,2},{2,3},{4,5},{5,6},{6,7},{8,9},{9,10},{10,11},{12,13},{... | collective-permute-start | bytes 1179656 | tf_op jit(solution)/shard_map/ppermute | solution.py:49
  289.6 16.5 %collective-permute-start.29 = (bf16[192,1024]{1,0:T(8,128)(2,1)S(1)}, bf16[192,1024]{1,0:T(8,128)(2,1)S(1)}, u32[]{:S(2)}, u32[]{:S(2)}) collective-permute-start(bf16[192,1024]{1,0:T(8,128)(2,1)S(1)} %get-tuple-element.39), channel_id=1, source_target_pairs={{1,0},{2,1},{3,2},{5,4},{6,5},{7,6},{9,8},{10,9},{11,10},{13,12},{... | collective-permute-start | bytes 1179656 | tf_op jit(solution)/shard_map/ppermute | solution.py:25
  294.3 15.8 %collective-permute-start.15 = (bf16[192,1024]{1,0:T(8,128)(2,1)S(1)}, bf16[192,1024]{1,0:T(8,128)(2,1)S(1)}, u32[]{:S(2)}, u32[]{:S(2)}) collective-permute-start(bf16[192,1024]{1,0:T(8,128)(2,1)S(1)} %collective-permute-done.14), channel_id=1, source_target_pairs={{1,2},{2,3},{5,6},{6,7},{9,10},{10,11},{13,14},{14,15},{17,18},{18... | collective-permute-start | bytes 1179656 | tf_op jit(solution)/shard_map/ppermute | solution.py:24
  297.7 16.4 %collective-permute-start.18 = (bf16[192,1024]{1,0:T(8,128)(2,1)S(1)}, bf16[192,1024]{1,0:T(8,128)(2,1)S(1)}, u32[]{:S(2)}, u32[]{:S(2)}) collective-permute-start(bf16[192,1024]{1,0:T(8,128)(2,1)S(1)} %collective-permute-done.17), channel_id=1, source_target_pairs={{1,0},{2,1},{5,4},{6,5},{9,8},{10,9},{13,12},{14,13},{17,16},{18,1... | collective-permute-start | bytes 1179656 | tf_op jit(solution)/shard_map/ppermute | solution.py:25
  301.7 16.8 %collective-permute-start.27 = (bf16[192,1024]{1,0:T(8,128)(2,1)S(1)}, bf16[192,1024]{1,0:T(8,128)(2,1)S(1)}, u32[]{:S(2)}, u32[]{:S(2)}) collective-permute-start(bf16[192,1024]{1,0:T(8,128)(2,1)S(1)} %collective-permute-done.26), channel_id=1, source_target_pairs={{1,2},{2,3},{5,6},{6,7},{9,10},{10,11},{13,14},{14,15},{17,18},{18... | collective-permute-start | bytes 1179656 | tf_op jit(solution)/shard_map/ppermute | solution.py:24
  306.1 16.4 %collective-permute-start.30 = (bf16[192,1024]{1,0:T(8,128)(2,1)S(1)}, bf16[192,1024]{1,0:T(8,128)(2,1)S(1)}, u32[]{:S(2)}, u32[]{:S(2)}) collective-permute-start(bf16[192,1024]{1,0:T(8,128)(2,1)S(1)} %collective-permute-done.29), channel_id=1, source_target_pairs={{1,0},{2,1},{5,4},{6,5},{9,8},{10,9},{13,12},{14,13},{17,16},{18,1... | collective-permute-start | bytes 1179656 | tf_op jit(solution)/shard_map/ppermute | solution.py:25
  310.1 17.1 %collective-permute-start.16 = (bf16[192,1024]{1,0:T(8,128)(2,1)S(1)}, bf16[192,1024]{1,0:T(8,128)(2,1)S(1)}, u32[]{:S(2)}, u32[]{:S(2)}) collective-permute-start(bf16[192,1024]{1,0:T(8,128)(2,1)S(1)} %collective-permute-done.15), channel_id=1, source_target_pairs={{2,3},{6,7},{10,11},{14,15},{18,19},{22,23},{26,27},{30,31}} | collective-permute-start | bytes 1179656 | tf_op jit(solution)/shard_map/ppermute | solution.py:24
  314.1 15.1 %collective-permute-start.19 = (bf16[192,1024]{1,0:T(8,128)(2,1)S(1)}, bf16[192,1024]{1,0:T(8,128)(2,1)S(1)}, u32[]{:S(2)}, u32[]{:S(2)}) collective-permute-start(bf16[192,1024]{1,0:T(8,128)(2,1)S(1)} %collective-permute-done.18), channel_id=1, source_target_pairs={{1,0},{5,4},{9,8},{13,12},{17,16},{21,20},{25,24},{29,28}} | collective-permute-start | bytes 1179656 | tf_op jit(solution)/shard_map/ppermute | solution.py:25
  355.9 15.7 %collective-permute-start.33 = (f32[2,16,8,128]{3,2,1,0:T(8,128)S(1)}, f32[2,16,8,128]{3,2,1,0:T(8,128)S(1)}, u32[]{:S(2)}, u32[]{:S(2)}) collective-permute-start(f32[2,16,8,128]{3,2,1,0:T(8,128)S(1)} %block_states.1), channel_id=1, source_target_pairs={{0,8},{4,12},{8,16},{12,20},{16,24},{20,28},{24,0},{28,4},{1,9},{5... | collective-permute-start | bytes 393224 | tf_op jit(solution)/shard_map/ppermute | solution.py:259
  367.4 16.8 %collective-permute-start.36 = (f32[2,16,8,128]{3,2,1,0:T(8,128)S(1)}, f32[2,16,8,128]{3,2,1,0:T(8,128)S(1)}, u32[]{:S(2)}, u32[]{:S(2)}) collective-permute-start(f32[2,16,8,128]{3,2,1,0:T(8,128)S(1)} %block_states.1), channel_id=1, source_target_pairs={{0,20},{4,24},{8,28},{12,0},{16,4},{20,8},{24,12},{28,16},{1,21},{... | collective-permute-start | bytes 393224 | tf_op jit(solution)/shard_map/ppermute | solution.py:259
  367.9 17.2 %collective-permute-start.37 = (f32[2,16,8,128]{3,2,1,0:T(8,128)S(1)}, f32[2,16,8,128]{3,2,1,0:T(8,128)S(1)}, u32[]{:S(2)}, u32[]{:S(2)}) collective-permute-start(f32[2,16,8,128]{3,2,1,0:T(8,128)S(1)} %block_states.1), channel_id=1, source_target_pairs={{0,24},{4,28},{8,0},{12,4},{16,8},{20,12},{24,16},{28,20},{1,25},{... | collective-permute-start | bytes 393224 | tf_op jit(solution)/shard_map/ppermute | solution.py:259
  371.6 16.1 %collective-permute-start.38 = (f32[2,16,8,128]{3,2,1,0:T(8,128)S(1)}, f32[2,16,8,128]{3,2,1,0:T(8,128)S(1)}, u32[]{:S(2)}, u32[]{:S(2)}) collective-permute-start(f32[2,16,8,128]{3,2,1,0:T(8,128)S(1)} %block_states.1), channel_id=1, source_target_pairs={{0,28},{4,0},{8,4},{12,8},{16,12},{20,16},{24,20},{28,24},{1,29},{... | collective-permute-start | bytes 393224 | tf_op jit(solution)/shard_map/ppermute | solution.py:259
  411.0 20.9 %collective-permute-start.45 = (bf16[192,1024]{1,0:T(8,128)(2,1)S(1)}, bf16[192,1024]{1,0:T(8,128)(2,1)S(1)}, u32[]{:S(2)}, u32[]{:S(2)}) collective-permute-start(bf16[192,1024]{1,0:T(8,128)(2,1)S(1)} %get-tuple-element.28), channel_id=1, source_target_pairs={{0,1},{4,5},{8,9},{12,13},{16,17},{20,21},{24,25},{28,29}} | collective-permute-start | bytes 1179656 | tf_op jit(solution)/shard_map/ppermute | solution.py:49
  412.3 21.7 %collective-permute-start.42 = (bf16[192,1024]{1,0:T(8,128)(2,1)S(1)}, bf16[192,1024]{1,0:T(8,128)(2,1)S(1)}, u32[]{:S(2)}, u32[]{:S(2)}) collective-permute-start(bf16[192,1024]{1,0:T(8,128)(2,1)S(1)} %get-tuple-element.25), channel_id=1, source_target_pairs={{3,2},{7,6},{11,10},{15,14},{19,18},{23,22},{27,26},{31,30}} | collective-permute-start | bytes 1179656 | tf_op jit(solution)/shard_map/ppermute | solution.py:50
  423.6 16.7 %collective-permute-start.40 = (bf16[192,1024]{1,0:T(8,128)(2,1)S(1)}, bf16[192,1024]{1,0:T(8,128)(2,1)S(1)}, u32[]{:S(2)}, u32[]{:S(2)}) collective-permute-start(bf16[192,1024]{1,0:T(8,128)(2,1)S(1)} %add_convert_fusion.9), channel_id=1, source_target_pairs={{0,1},{1,2},{4,5},{5,6},{8,9},{9,10},{12,13},{13,14},{16,17},{17,1... | collective-permute-start | bytes 1179656 | tf_op jit(solution)/shard_map/ppermute | solution.py:49
  425.5 16.5 %collective-permute-start.48 = (bf16[192,1024]{1,0:T(8,128)(2,1)S(1)}, bf16[192,1024]{1,0:T(8,128)(2,1)S(1)}, u32[]{:S(2)}, u32[]{:S(2)}) collective-permute-start(bf16[192,1024]{1,0:T(8,128)(2,1)S(1)} %get-tuple-element.29), channel_id=1, source_target_pairs={{3,2},{7,6},{11,10},{15,14},{19,18},{23,22},{27,26},{31,30}} | collective-permute-start | bytes 1179656 | tf_op jit(solution)/shard_map/ppermute | solution.py:50
  432.0 16.0 %collective-permute-start.46 = (bf16[192,1024]{1,0:T(8,128)(2,1)S(1)}, bf16[192,1024]{1,0:T(8,128)(2,1)S(1)}, u32[]{:S(2)}, u32[]{:S(2)}) collective-permute-start(bf16[192,1024]{1,0:T(8,128)(2,1)S(1)} %add_convert_fusion.4), channel_id=1, source_target_pairs={{0,1},{1,2},{4,5},{5,6},{8,9},{9,10},{12,13},{13,14},{16,17},{17,1... | collective-permute-start | bytes 1179656 | tf_op jit(solution)/shard_map/ppermute | solution.py:49
  454.5 16.4 %collective-permute-start.44 = (bf16[192,1024]{1,0:T(8,128)(2,1)S(1)}, bf16[192,1024]{1,0:T(8,128)(2,1)S(1)}, u32[]{:S(2)}, u32[]{:S(2)}) collective-permute-start(bf16[192,1024]{1,0:T(8,128)(2,1)S(1)} %add_convert_fusion.6), channel_id=1, source_target_pairs={{1,0},{2,1},{3,2},{5,4},{6,5},{7,6},{9,8},{10,9},{11,10},{13,12},{... | collective-permute-start | bytes 1179656 | tf_op jit(solution)/shard_map/ppermute | solution.py:50
  462.6 15.1 %collective-permute-start.50 = (bf16[192,1024]{1,0:T(8,128)(2,1)S(1)}, bf16[192,1024]{1,0:T(8,128)(2,1)S(1)}, u32[]{:S(2)}, u32[]{:S(2)}) collective-permute-start(bf16[192,1024]{1,0:T(8,128)(2,1)S(1)} %add_convert_fusion.1), channel_id=1, source_target_pairs={{1,0},{2,1},{3,2},{5,4},{6,5},{7,6},{9,8},{10,9},{11,10},{13,12},{... | collective-permute-start | bytes 1179656 | tf_op jit(solution)/shard_map/ppermute | solution.py:50
  (38 other events, 633.2 us)
Sparse Core Ops, SparseCore 0:
  11.4 130.4 all-gather.4
  143.8 57.1 all-gather.6
  202.8 130.2 all-gather.8
  334.9 67.1 all-gather.10
